TPU v7x, 128 devices: a whole 4x4x4 slice. The times are simulated.
128 devices in a mesh: bl: 8 (over x, core), ma: 16 (over z, y).
Axes of the slice: x: 4, y: 4, z: 4, core: 2. Of those that a mesh axis runs over, the one named last changes fastest.
Arguments:
- beam_fringe_harmonics: bfloat16 [128, 32, 2, 1024], P('bl'), may hold values from -6 to 6
- legendre: bfloat16 [32, 1536, 1024], P(None, 'ma'), may hold values from -0.1875 to 0.1875
- visibility: float32 [128, 2, 4096], P('bl', None, 'ma'), may hold values from -6 to 6
- owner_orders: int32 [16, 4], replicated, may hold values from 0 to 32, as said below
Outputs:
- normal: bfloat16 [64, 2, 1536, 1536], P('ma', None, 'bl')
- dirty_map: float32 [64, 2, 1536], P('ma', None, 'bl')
Inputs may be any that keep to these rules, and one draw needn't show every extreme that they name: `owner_orders`: row k lists the orders that owner k holds in its first slots; each of the 32 orders stands in exactly one slot and the other slots hold 32. Owners hold from 0 to 4 orders, and in every draw some owner holds 4 and some none.
All inputs are finite; a program needn't handle non-finite values.
Results may differ from a plain program's by a relative error of at most 0.0056.
Values may be sent and summed in bfloat16 or wider, within the bound.
A program may use at most 64 MiB of HBM per device.

v0:
```python
import math

import jax
import jax.numpy as jnp
from jax import lax
from jax.sharding import PartitionSpec as P


def sidereal_transform(series, total_time, orders, order_limit):
    times = jnp.arange(series.shape[2], dtype=jnp.int32)
    clipped = jnp.minimum(orders, order_limit - 1)
    phases = times[:, None] * clipped[None, :] % total_time
    angles = phases.astype(jnp.float32) * (2.0 * math.pi / total_time)
    cosine = jnp.cos(angles)
    sine_table = jnp.sin(angles)
    usable = (orders < order_limit).astype(jnp.float32) / math.sqrt(total_time)
    real_in = series[:, 0, :]
    imag_in = series[:, 1, :]
    maximum_degree = lax.Precision.HIGHEST
    real_out = (
        jnp.dot(real_in, cosine, precision=maximum_degree)
        + jnp.dot(imag_in, sine_table, precision=maximum_degree)
    ) * usable
    imag_out = (
        jnp.dot(imag_in, cosine, precision=maximum_degree)
        - jnp.dot(real_in, sine_table, precision=maximum_degree)
    ) * usable
    return jnp.stack([real_out, imag_out], axis=2).transpose(1, 0, 2)


def on_device(beam_fringe_harmonics, legendre, visibility, owner_orders):
    holder_device_total = lax.axis_size("ma")
    segment_total = lax.axis_size("bl")
    owner_index = lax.axis_index("ma")
    row_index = lax.axis_index("bl")
    bucket_room = owner_orders.shape[1]
    order_total = beam_fringe_harmonics.shape[1]
    local_antenna_pairs = beam_fringe_harmonics.shape[0]
    antenna_pair_count_total = local_antenna_pairs * segment_total
    multipole_count = legendre.shape[1] * holder_device_total
    row_count = multipole_count // segment_total
    row_start = row_index * row_count
    time_local = visibility.shape[2]
    total_time = time_local * holder_device_total
    orders_all = owner_orders.reshape(-1)
    harmonic = lax.dot_general(
        beam_fringe_harmonics,
        legendre,
        (((3,), (2,)), ((1,), (0,))),
        preferred_element_type=jnp.float32,
    ).astype(jnp.bfloat16)
    select = (orders_all[:, None] == jnp.arange(order_total, dtype=jnp.int32)[None, :]).astype(
        jnp.bfloat16
    )
    flat_blocks = harmonic.reshape(order_total, -1)
    departing_parts = jnp.dot(select, flat_blocks, preferred_element_type=jnp.float32).astype(
        jnp.bfloat16
    )
    departing_parts = departing_parts.reshape(
        holder_device_total, bucket_room, local_antenna_pairs, 2, -1
    )
    whole_day = lax.all_gather(visibility, "ma", axis=2, tiled=True)
    own_orders = lax.dynamic_slice_in_dim(owner_orders, owner_index, 1, 0).reshape(-1)
    own_spectra = sidereal_transform(whole_day, total_time, own_orders, order_total).astype(
        jnp.bfloat16
    )
    tiled_blocks = jnp.broadcast_to(
        departing_parts[None], (segment_total,) + departing_parts.shape
    ).reshape((segment_total * holder_device_total,) + departing_parts.shape[1:])
    incoming_parts = lax.all_to_all(
        tiled_blocks, ("bl", "ma"), split_axis=0, concat_axis=4, tiled=True
    )[0]
    incoming_parts = incoming_parts.reshape(
        bucket_room, local_antenna_pairs, 2, segment_total, multipole_count
    )
    incoming_parts = incoming_parts.transpose(0, 3, 1, 2, 4).reshape(
        bucket_room, antenna_pair_count_total, 2, multipole_count
    )
    spectra_every = lax.all_gather(own_spectra, "bl", axis=1, tiled=True)
    block_of_rows = lax.dynamic_slice_in_dim(incoming_parts, row_start, row_count, 3)
    real_rows = jnp.einsum(
        "sbkr,sbkc->src", block_of_rows, incoming_parts, preferred_element_type=jnp.float32
    )
    imag_rows = jnp.einsum(
        "pmt,pmx->ptx",
        block_of_rows[:, :, 0],
        incoming_parts[:, :, 1],
        preferred_element_type=jnp.float32,
    )
    imag_rows = imag_rows - jnp.einsum(
        "pmt,pmx->ptx",
        block_of_rows[:, :, 1],
        incoming_parts[:, :, 0],
        preferred_element_type=jnp.float32,
    )
    padded_rows = block_of_rows.astype(jnp.float32)
    padded_spectra = spectra_every.astype(jnp.float32)
    maximum_degree = lax.Precision.HIGHEST
    dirty_real = jnp.einsum(
        "ieg,ie->ig", padded_rows[:, :, 0], padded_spectra[:, :, 0], precision=maximum_degree
    ) + jnp.einsum(
        "ieg,ie->ig", padded_rows[:, :, 1], padded_spectra[:, :, 1], precision=maximum_degree
    )
    dirty_imag = jnp.einsum(
        "ieg,ie->ig", padded_rows[:, :, 0], padded_spectra[:, :, 1], precision=maximum_degree
    ) - jnp.einsum(
        "ieg,ie->ig", padded_rows[:, :, 1], padded_spectra[:, :, 0], precision=maximum_degree
    )
    normal = (jnp.stack([real_rows, imag_rows], axis=1) / antenna_pair_count_total).astype(
        jnp.bfloat16
    )
    dirty_map = jnp.stack([dirty_real, dirty_imag], axis=1) / math.sqrt(antenna_pair_count_total)
    return (normal, dirty_map)


def solution(mesh):
    return jax.shard_map(
        on_device,
        mesh=mesh,
        in_specs=(P("bl", None, None, None), P(None, "ma", None), P("bl", None, "ma"), P()),
        out_specs=(P("ma", None, "bl", None), P("ma", None, "bl")),
        check_vma=False,
    )
```

profile of v0, /device:TPU:1, one launch (start us, length us, event | category | flops | bytes accessed | tf_op | source)
XLA Modules:
  0.0 136.4 jit_solution(9200096475862339537)
XLA Ops:
  0.6 0.8 copy.49
  1.5 5.8 %fusion.5 = bf16[32,16,2,96]{3,1,2,0:T(8,128)(2,1)S(1)} fusion(bf16[32,96,1024]{2,1,0:T(8,128)(2,1)} %param.5, bf16[16,32,2,1024]{3,2,1,0:T(2,128)(2,1)} %param.4), kind=kOutput, calls=%fused_computation.11 | convolution fusion | flops 201424896 | bytes 8585216 | tf_op jit(solution)/shard_map/dot_general | solution.py:46
  7.3 0.2 copy.51
  7.5 0.3 reshape.17
  7.9 0.3 convolution_convert_fusion
  8.2 0.5 broadcast_in_dim.4
  8.7 6.3 %broadcast_in_dim.5 = bf16[8,16,4,16,2,96]{5,4,3,2,1,0:T(2,128)(2,1)} broadcast(bf16[16,4,16,2,96]{4,3,2,1,0:T(2,128)(2,1)S(1)} %broadcast_in_dim.4), dimensions={1,2,3,4,5} | broadcast | bytes 3538944 | tf_op jit(solution)/shard_map/broadcast_in_dim | solution.py:67
  15.0 12.0 %all-to-all-start = ((bf16[128,4,16,2,96]{4,3,2,1,0:T(2,128)(2,1)}), bf16[128,4,16,2,96]{4,3,2,1,0:T(2,128)(2,1)}, u32[]{:S(2)}, u32[]{:S(2)}) async-start(bf16[128,4,16,2,96]{4,3,2,1,0:T(2,128)(2,1)} %bitcast.86), calls=%async_computation | async-start | bytes 8388608 | tf_op jit(solution)/shard_map/all_to_all | solution.py:70
  27.0 0.2 minimum_reduce_fusion
  27.2 0.2 select_reduce_fusion
  27.4 60.1 %all_gather.6 = f32[16,2,4096]{2,0,1:T(8,128)S(1)} all-gather(f32[16,2,256]{2,0,1:T(8,128)S(1)} %copy.57), channel_id=1, replica_groups=mesh['bl'=8,'ma'=16] {'ma'}, dimensions={2}, use_global_device_ids=true | all-gather | bytes 557056 | tf_op jit(solution)/shard_map/all_gather | solution.py:62
  87.4 0.9 fusion.18
  88.4 1.0 fusion.14
  89.3 0.9 fusion.17
  90.3 1.0 fusion.15
  91.2 0.1 copy.58
  91.4 18.7 %all_gather.7 = bf16[4,128,2]{0,2,1:T(2,128)(2,1)S(1)} all-gather(bf16[4,16,2]{0,2,1:T(2,128)(2,1)S(1)} %copy.58), channel_id=1, replica_groups=mesh['bl'=8,'ma'=16] {'bl'}, dimensions={1}, use_global_device_ids=true | all-gather | bytes 2304 | tf_op jit(solution)/shard_map/all_gather | solution.py:79
  110.0 0.1 fusion.58
  110.2 0.1 copy.68
  110.3 9.1 %copy.52 = bf16[1,4,16,2,128,96]{5,4,3,2,1,0:T(8,128)(2,1)} copy(bf16[1,4,16,2,128,96]{5,3,2,1,4,0:T(2,128)(2,1)} %bitcast.4) | data formatting | bytes 6291456 | tf_op jit(solution)/shard_map/all_to_all | solution.py:70
  119.4 6.8 %reshape_squeeze.3 = bf16[4,16,2,8,1536]{4,3,2,1,0:T(8,128)(2,1)S(1)} reshape(bf16[1,4,16,2,128,96]{5,4,3,2,1,0:T(8,128)(2,1)} %copy.52) | data formatting | bytes 6291456 | tf_op jit(solution)/shard_map/reshape;squeeze | solution.py:73
  126.2 1.7 %copy.53 = bf16[4,8,16,2,1536]{4,2,1,3,0:T(8,128)(2,1)S(1)} copy(bf16[4,8,16,2,1536]{4,1,3,2,0:T(8,128)(2,1)S(1)} %bitcast.87) | data formatting | bytes 6291456 | tf_op jit(solution)/shard_map/transpose | solution.py:76
  127.9 0.3 fusion.20
  128.2 0.3 fusion.21
  128.4 0.3 fusion.19
  128.7 0.3 fusion.22
  129.0 0.9 fusion.4
  129.9 0.9 convolution_bitcast_fusion
  130.8 0.6 copy.62
  131.4 0.9 subtract_bitcast_fusion
  132.3 1.3 fusion
  133.7 2.7 %copy.61 = bf16[4,2,192,1536]{3,2,1,0:T(8,128)(2,1)} copy(bf16[4,2,192,1536]{3,2,0,1:T(8,128)(2,1)S(1)} %fusion) | data formatting | bytes 9437184
  (11 shorter events, 0.2 us)
Async XLA Ops:
  15.0 12.0 %copy-start = (f32[16,2,256]{2,1,0:T(2,128)S(1)}, f32[16,2,256]{2,1,0:T(2,128)}, u32[]{:S(2)}) copy-start(f32[16,2,256]{2,1,0:T(2,128)} %param.6) | copy-start | bytes 98308
  15.0 12.0 %copy-start.1 = (s32[16,4]{0,1:T(4,128)S(1)}, s32[16,4]{0,1:T(4,128)}, u32[]{:S(2)}) copy-start(s32[16,4]{0,1:T(4,128)} %param.7) | copy-start | bytes 772
  15.0 95.3 %all-to-all-start = ((bf16[128,4,16,2,96]{4,3,2,1,0:T(2,128)(2,1)}), bf16[128,4,16,2,96]{4,3,2,1,0:T(2,128)(2,1)}, u32[]{:S(2)}, u32[]{:S(2)}) async-start(bf16[128,4,16,2,96]{4,3,2,1,0:T(2,128)(2,1)} %bitcast.86), calls=%async_computation | async-start | bytes 8388608 | tf_op jit(solution)/shard_map/all_to_all | solution.py:70
where the time goes:
time: 137 us; the launch traced here: 136 us
  blocking collectives  78.7 us (57%)
  local copies, waits for them, and re-layouts  29.5 us (22%)
  matrix products  13.7 us (10%)
  starting transfers between devices  12 us (9%)
  other arithmetic  1.74 us (1%)
    all_gather x1, blocking collectives, on_device(): whole_day = lax.all_gather(visibility, 'ma', axis=2, tiled=True)  60.1 us
    all_gather x1, blocking collectives, on_device(): spectra_every = lax.all_gather(own_spectra, 'bl', axis=1, tiled=True)  18.7 us
    all_to_all x1, starting transfers between devices, on_device(): lax.all_to_all(tiled_blocks, ('bl', 'ma'), split_axis=0, concat_axis=4, t...  12 us
    all_to_all x1, local copies, waits for them, and re-layouts, on_device(): lax.all_to_all(tiled_blocks, ('bl', 'ma'), split_axis=0, concat_axis=4, t...  9.08 us
    broadcast_in_dim x2, local copies, waits for them, and re-layouts, on_device(): jnp.broadcast_to(departing_parts[None], (segment_total,) + departing_part...  6.83 us
    another operation x1, local copies, waits for them, and re-layouts, on_device(): incoming_parts.reshape(bucket_room, local_antenna_pairs, 2, segment_total...  6.77 us
    dot_general x1, matrix products, on_device(): lax.dot_general(beam_fringe_harmonics, legendre, (((3,), (2,)), ((1,), (0...  5.83 us
    unnamed x8, local copies, waits for them, and re-layouts  4.07 us
  transfers between devices with their start and end apart: 1, of which 0 were waited for; matrix products, arithmetic and copies ran while one was open for 3% of the time, Pallas kernels for 0%

commit v1 on v0

v1 whole, which is shorter than its diff:
```python
import functools
import math

import jax
import jax.numpy as jnp
from jax import lax
from jax.experimental import pallas as pl
from jax.experimental.pallas import tpu as pltpu
from jax.sharding import PartitionSpec as P

F32 = jnp.float32
BF16 = jnp.bfloat16
MESH = pl.DeviceIdType.MESH

NZ = 4
NY = 4
NX = 4
CAP = 4
ORDERS = 32
DEG = 96
PACK = 112
ROWS = 32
COLS = 1536
GROUP = 8
RELATIVE = (0, 1, 3, 2)


def gather_kernel(
    orders_ref, legendre_ref, beam_ref, visibility_ref,
    blocks_ref, spectra_ref,
    legendre, beam, harmonic, outgoing, arrived, held, spectra,
    load_sem, beam_sem, a_send, a_recv, x_send, x_recv, c_send, c_recv, s_send, s_recv, out_sem,
):
    bl = lax.axis_index("bl")
    ma = lax.axis_index("ma")
    x, core = bl // 2, bl % 2
    z, y = ma // NY, ma % NY
    right = ((x + 1) % NX) * 2 + core
    left = ((x + NX - 1) % NX) * 2 + core
    across = ((x + 2) % NX) * 2 + core
    sibling = x * 2 + (1 - core)

    beam_load = pltpu.make_async_copy(beam_ref, beam, beam_sem)
    beam_load.start()
    loads = []
    for g in range(ORDERS // GROUP):
        part = pl.ds(g * GROUP, GROUP)
        load = pltpu.make_async_copy(legendre_ref.at[part], legendre.at[part], load_sem.at[g])
        load.start()
        loads.append(load)

    barrier = pltpu.get_barrier_semaphore()
    for dz in range(NZ):
        for dy in range(NY):
            if dz or dy:
                peer = ((z + dz) % NZ) * NY + (y + dy) % NY
                pl.semaphore_signal(barrier, inc=1, device_id={"bl": bl, "ma": peer}, device_id_type=MESH)
    for d in range(1, 2 * NX):
        pl.semaphore_signal(
            barrier, inc=1, device_id={"bl": (bl + d) % (2 * NX), "ma": ma}, device_id_type=MESH
        )

    times = visibility_ref.shape[2]
    total_time = times * NZ * NY
    order_index = lax.broadcasted_iota(jnp.int32, (ORDERS, times), 0)
    time_index = lax.broadcasted_iota(jnp.int32, (ORDERS, times), 1) + ma * times
    angle = ((order_index * time_index) & (total_time - 1)).astype(F32) * (2.0 * math.pi / total_time)
    cosine, sine = jnp.cos(angle), jnp.sin(angle)
    real = visibility_ref[:, 0, :]
    imag = visibility_ref[:, 1, :]
    direct = jnp.concatenate([real, imag] * CAP, axis=0)
    turned = jnp.concatenate([imag, -real] * CAP, axis=0)
    contract = (((1,), (1,)), ((), ()))
    partial = (
        lax.dot_general(cosine, direct, contract, precision=lax.Precision.HIGHEST, preferred_element_type=F32)
        + lax.dot_general(sine, turned, contract, precision=lax.Precision.HIGHEST, preferred_element_type=F32)
    ) * (1.0 / math.sqrt(total_time))
    high = partial.astype(BF16).astype(F32)
    low = partial - high
    row = lax.broadcasted_iota(jnp.int32, (PACK - DEG, 128), 0)
    for m in range(ORDERS):
        harmonic[m, DEG:PACK, :] = jnp.where(
            row == 0, high[m : m + 1], jnp.where(row == 1, low[m : m + 1], 0.0)
        ).astype(BF16)
    harmonic[ORDERS] = jnp.zeros((PACK, 128), BF16)

    lane = lax.broadcasted_iota(jnp.int32, (DEG, 128), 1) // ROWS
    beam_load.wait()
    for g in range(ORDERS // GROUP):
        loads[g].wait()
        part = pl.ds(g * GROUP, GROUP)
        product = lax.dot_general(
            legendre[part].reshape(GROUP * DEG, -1),
            beam[part].reshape(GROUP * ROWS, -1),
            contract,
            preferred_element_type=F32,
        )
        for i in range(GROUP):
            half = (i * ROWS) // 128
            own = product[i * DEG : (i + 1) * DEG, half * 128 : (half + 1) * 128]
            own = jnp.where(lane == i % (128 // ROWS), own, 0.0)
            own = own + pltpu.roll(own, ROWS, 1)
            own = own + pltpu.roll(own, 2 * ROWS, 1)
            harmonic[g * GROUP + i, 0:DEG, :] = own.astype(BF16)

    pl.semaphore_wait(barrier, NZ * NY - 1 + 2 * NX - 1)

    slot_lane = lax.broadcasted_iota(jnp.int32, (PACK, 128), 1) // ROWS
    exchange = []
    for t in range(NZ):
        for dy in range(NY):
            n = t * NY + dy
            owner = ((z + NZ - RELATIVE[t]) % NZ) * NY + (y + dy) % NY
            parts = [harmonic[orders_ref[owner * CAP + s]] for s in range(CAP)]
            block = jnp.where(
                slot_lane < 2,
                jnp.where(slot_lane == 0, parts[0], parts[1]),
                jnp.where(slot_lane == 2, parts[2], parts[3]),
            )
            if n == 0:
                arrived[ma] = block
                exchange.append(None)
            else:
                outgoing[n] = block
                copy = pltpu.make_async_remote_copy(
                    src_ref=outgoing.at[n],
                    dst_ref=arrived.at[ma],
                    send_sem=a_send.at[n],
                    recv_sem=a_recv.at[n],
                    device_id={"bl": bl, "ma": owner},
                    device_id_type=MESH,
                )
                copy.start()
                exchange.append(copy)

    sent = []

    def view(t, who, first=0, count=ROWS):
        zs = (z + RELATIVE[t]) % NZ
        start = pl.multiple_of(who * ROWS + first, 16)
        return held.at[:, pl.ds(start, count), pl.ds(pl.multiple_of(zs * (NY * DEG), 128), NY * DEG)]

    def send(ref, to, send_sem, recv_sem):
        copy = pltpu.make_async_remote_copy(
            src_ref=ref, dst_ref=ref, send_sem=send_sem, recv_sem=recv_sem,
            device_id={"bl": to, "ma": ma}, device_id_type=MESH,
        )
        copy.start()
        sent.append(copy)

    def await_view(ref, recv_sem):
        pltpu.make_async_copy(ref, ref, recv_sem).wait()

    def own_part(t):
        for dy in range(NY):
            if t or dy:
                exchange[t * NY + dy].wait_recv()
        zs = (z + RELATIVE[t]) % NZ
        stacked = jnp.concatenate([arrived[zs * NY + j, 0:DEG, :] for j in range(NY)], axis=0)
        held[:, pl.ds(pl.multiple_of(bl * ROWS, 16), ROWS),
             pl.ds(pl.multiple_of(zs * (NY * DEG), 128), NY * DEG)] = stacked.T.reshape(CAP, ROWS, NY * DEG)
        send(view(t, bl), right, x_send.at[t, 0], x_recv.at[t, 0])
        send(view(t, bl), left, x_send.at[t, 1], x_recv.at[t, 1])
        send(view(t, bl), sibling, c_send.at[t, 0], c_recv.at[t, 0])

    def near_part(t):
        await_view(view(t, left), x_recv.at[t, 0])
        send(view(t, left, 0, ROWS // 2), right, x_send.at[t, 2], x_recv.at[t, 2])
        send(view(t, left), sibling, c_send.at[t, 1], c_recv.at[t, 1])
        await_view(view(t, right), x_recv.at[t, 1])
        send(view(t, right, ROWS // 2, ROWS // 2), left, x_send.at[t, 3], x_recv.at[t, 3])
        send(view(t, right), sibling, c_send.at[t, 2], c_recv.at[t, 2])

    def far_part(t):
        await_view(view(t, across, 0, ROWS // 2), x_recv.at[t, 2])
        await_view(view(t, across, ROWS // 2, ROWS // 2), x_recv.at[t, 3])
        send(view(t, across), sibling, c_send.at[t, 3], c_recv.at[t, 3])

    own_part(0)
    own_part(1)
    near_part(0)
    own_part(2)
    near_part(1)
    far_part(0)
    own_part(3)

    total = jnp.zeros((PACK - DEG, 128), F32)
    for k in range(NZ * NY):
        total = total + arrived[k, DEG:PACK, :].astype(F32)
    line = jnp.sum(total, axis=0, keepdims=True).astype(BF16).astype(F32)
    spectra[bl] = jnp.broadcast_to(line, (8, 128))
    spectra_sent = []
    for d in range(1, 2 * NX):
        copy = pltpu.make_async_remote_copy(
            src_ref=spectra.at[bl], dst_ref=spectra.at[bl], send_sem=s_send.at[d], recv_sem=s_recv.at[d],
            device_id={"bl": (bl + d) % (2 * NX), "ma": ma}, device_id_type=MESH,
        )
        copy.start()
        spectra_sent.append(copy)

    near_part(2)
    far_part(1)
    near_part(3)
    far_part(2)
    far_part(3)

    other = 1 - 2 * core
    for t in range(NZ):
        await_view(view(t, bl + other), c_recv.at[t, 0])
        await_view(view(t, left + other), c_recv.at[t, 1])
        await_view(view(t, right + other), c_recv.at[t, 2])
        await_view(view(t, across + other), c_recv.at[t, 3])
    for d in range(1, 2 * NX):
        spectra_sent[d - 1].wait_recv()
    out = pltpu.make_async_copy(held, blocks_ref, out_sem.at[0])
    out.start()
    out2 = pltpu.make_async_copy(spectra, spectra_ref, out_sem.at[1])
    out2.start()
    for copy in exchange[1:]:
        copy.wait_send()
    for copy in sent + spectra_sent:
        copy.wait_send()
    out.wait()
    out2.wait()


def gather(orders, legendre, beam, visibility):
    any_spec = pl.BlockSpec(memory_space=pl.ANY)
    dma = pltpu.SemaphoreType.DMA
    return pl.pallas_call(
        gather_kernel,
        out_shape=(
            jax.ShapeDtypeStruct((CAP, 2 * NX * ROWS, COLS), BF16),
            jax.ShapeDtypeStruct((2 * NX, 8, 128), F32),
        ),
        in_specs=[
            pl.BlockSpec(memory_space=pltpu.SMEM),
            any_spec,
            any_spec,
            pl.BlockSpec(memory_space=pltpu.VMEM),
        ],
        out_specs=(any_spec, any_spec),
        scratch_shapes=[
            pltpu.VMEM(legendre.shape, BF16),
            pltpu.VMEM(beam.shape, BF16),
            pltpu.VMEM((ORDERS + 1, PACK, 128), BF16),
            pltpu.VMEM((NZ * NY, PACK, 128), BF16),
            pltpu.VMEM((NZ * NY, PACK, 128), BF16),
            pltpu.VMEM((CAP, 2 * NX * ROWS, COLS), BF16),
            pltpu.VMEM((2 * NX, 8, 128), F32),
            dma((ORDERS // GROUP,)),
            dma,
            dma((NZ * NY,)),
            dma((NZ * NY,)),
            dma((NZ, 4)),
            dma((NZ, 4)),
            dma((NZ, 4)),
            dma((NZ, 4)),
            dma((2 * NX,)),
            dma((2 * NX,)),
            dma((2,)),
        ],
        compiler_params=pltpu.CompilerParams(
            collective_id=0, has_side_effects=True, vmem_limit_bytes=40 * 1024 * 1024
        ),
        name="gather_blocks",
    )(orders, legendre, beam, visibility)


def normal_kernel(blocks_ref, spectra_ref, normal_ref, map_ref, turned, own):
    s = pl.program_id(0)
    bl = lax.axis_index("bl")
    start = pl.multiple_of(((3 * bl) // 2) * 128, 128)
    skip = pl.multiple_of((bl % 2) * 64, 16)
    window = blocks_ref[0, :, pl.ds(start, 256)]
    pieces = []
    for k in range(2 * NX):
        pieces.append(-window[k * ROWS + ROWS // 2 : (k + 1) * ROWS])
        pieces.append(window[k * ROWS : k * ROWS + ROWS // 2])
    own[...] = window.T
    turned[...] = jnp.concatenate(pieces, axis=0).T
    left = jnp.concatenate([own[pl.ds(skip, 192), :], turned[pl.ds(skip, 192), :]], axis=0)
    scale = 1.0 / 128.0
    for n in range(COLS // 256):
        part = pl.ds(n * 256, 256)
        product = jnp.dot(left, blocks_ref[0, :, part], preferred_element_type=F32) * scale
        normal_ref[0, 0, :, part] = product[0:192].astype(BF16)
        normal_ref[0, 1, :, part] = product[192:384].astype(BF16)
    lane = lax.broadcasted_iota(jnp.int32, (8, 128), 1) // ROWS
    halves = []
    for h in range(2):
        line = jnp.zeros((8, 128), F32)
        for q in range(4):
            moved = pltpu.roll(spectra_ref[h * 4 + q], (q * ROWS + 128 - s * ROWS) % 128, 1)
            line = jnp.where(lane == q, moved, line)
        halves.append(line)
    spectrum = jnp.concatenate(halves, axis=1).astype(BF16)
    adjoint = lax.dot_general(spectrum, left, (((1,), (1,)), ((), ())), preferred_element_type=F32)
    adjoint = adjoint * (1.0 / math.sqrt(128.0))
    map_ref[0, 0:1, :] = adjoint[0:1, 0:192]
    map_ref[0, 1:2, :] = adjoint[0:1, 192:384]


def normal_maps(blocks, spectra):
    return pl.pallas_call(
        normal_kernel,
        grid=(CAP,),
        out_shape=(
            jax.ShapeDtypeStruct((CAP, 2, 192, COLS), BF16),
            jax.ShapeDtypeStruct((CAP, 2, 192), F32),
        ),
        in_specs=[
            pl.BlockSpec((1, 256, COLS), lambda s: (s, 0, 0)),
            pl.BlockSpec((2 * NX, 8, 128), lambda s: (0, 0, 0)),
        ],
        out_specs=(
            pl.BlockSpec((1, 2, 192, COLS), lambda s: (s, 0, 0, 0)),
            pl.BlockSpec((1, 2, 192), lambda s: (s, 0, 0)),
        ),
        scratch_shapes=[pltpu.VMEM((256, 256), BF16), pltpu.VMEM((256, 256), BF16)],
        compiler_params=pltpu.CompilerParams(vmem_limit_bytes=40 * 1024 * 1024),
        name="normal_maps",
    )(blocks, spectra)


def on_device(beam_fringe_harmonics, legendre, visibility, owner_orders):
    beam = beam_fringe_harmonics.transpose(1, 2, 0, 3).reshape(ORDERS, ROWS, -1)
    blocks, spectra = gather(owner_orders.reshape(-1), legendre, beam, visibility)
    return normal_maps(blocks, spectra)


def solution(mesh):
    return jax.shard_map(
        on_device,
        mesh=mesh,
        in_specs=(P("bl", None, None, None), P(None, "ma", None), P("bl", None, "ma"), P()),
        out_specs=(P("ma", None, "bl", None), P("ma", None, "bl")),
        check_vma=False,
    )
```

time: 137 us -> 45.8 us (0.33)
  blocking collectives: 78.7 us -> 0 us
  Pallas kernels: 0 us -> 37.9 us
  local copies, waits for them, and re-layouts: 29.5 us -> 6.95 us
  matrix products: 13.7 us -> 0 us
  starting transfers between devices: 12 us -> 0 us
  other arithmetic: 1.74 us -> 0 us
    all_gather x2 -> x0, blocking collectives: 78.7 us -> none  [the longest x1 60.1 us: on_device(): whole_day = lax.all_gather(visibility, 'ma', axis=2, tiled=True)]
    pallas_call x0 -> x2, Pallas kernels: none -> 37.9 us  [the longest x1 34.2 us: gather(): pl.pallas_call(gather_kernel, out_shape=(jax.ShapeDtypeStruct((CAP, 2 * N...]
    dot_general x13 -> x0, matrix products: 13.7 us -> none  [the longest x1 5.83 us: on_device(): lax.dot_general(beam_fringe_harmonics, legendre, (((3,), (2,)), ((1,), (0...]
    all_to_all x1 -> x0, starting transfers between devices: 12 us -> none  [on_device(): lax.all_to_all(tiled_blocks, ('bl', 'ma'), split_axis=0, concat_axis=4, t...]
    all_to_all x1 -> x0, local copies, waits for them, and re-layouts: 9.08 us -> none  [on_device(): lax.all_to_all(tiled_blocks, ('bl', 'ma'), split_axis=0, concat_axis=4, t...]
    broadcast_in_dim x2 -> x0, local copies, waits for them, and re-layouts: 6.83 us -> none  [on_device(): jnp.broadcast_to(departing_parts[None], (segment_total,) + departing_part...]
    another operation x1 -> x0, local copies, waits for them, and re-layouts: 6.77 us -> none  [on_device(): incoming_parts.reshape(bucket_room, local_antenna_pairs, 2, segment_total...]
    transpose x1, local copies, waits for them, and re-layouts: 1.73 us -> 3.32 us  [on_device(): beam = beam_fringe_harmonics.transpose(1, 2, 0, 3).reshape(ORDERS, ROWS, -1)]
  transfers between devices with their start and end apart: 1 -> 0, of which waited for: 0 -> 0; matrix products, arithmetic and copies ran while one was open for 3% -> 0% of each run, Pallas kernels for 0% -> 0%
where the time goes in v1:
time: 45.8 us; the launch traced here: 45.6 us
  Pallas kernels  37.9 us (83%)
  local copies, waits for them, and re-layouts  6.95 us (15%)
  between operations  0.67 us (1%)
    pallas_call x1, Pallas kernels, gather(): pl.pallas_call(gather_kernel, out_shape=(jax.ShapeDtypeStruct((CAP, 2 * N...  34.2 us
    pallas_call x1, Pallas kernels, normal_maps(): pl.pallas_call(normal_kernel, grid=(CAP,), out_shape=(jax.ShapeDtypeStruc...  3.77 us
    unnamed x5, local copies, waits for them, and re-layouts  3.55 us
    transpose x1, local copies, waits for them, and re-layouts, on_device(): beam = beam_fringe_harmonics.transpose(1, 2, 0, 3).reshape(ORDERS, ROWS, -1)  3.32 us

profile of v1, /device:TPU:1, one launch (start us, length us, event | category | flops | bytes accessed | tf_op | source)
XLA Modules:
  0.0 45.6 jit_solution(186726871139918963)
XLA Ops:
  0.6 0.0 copy-start.1
  0.6 0.8 %copy.8 = s32[16,4]{1,0:T(8,128)S(1)} copy(s32[16,4]{0,1:T(4,128)} %param.7) | data formatting | bytes 512 | tf_op args[3]
  1.4 0.1 reshape.10.orders_ref
  1.5 3.3 %copy.9 = bf16[32,2,16,1024]{3,2,1,0:T(8,128)(2,1)S(1)} copy(bf16[32,2,16,1024]{3,1,0,2:T(2,128)(2,1)} %bitcast.3) | data formatting | bytes 4194304 | tf_op jit(solution)/shard_map/transpose | solution.py:327
  4.8 0.0 copy-done.1
  4.8 0.0 copy-start
  4.8 2.8 %copy-done = bf16[32,96,1024]{2,1,0:T(8,128)(2,1)S(1)} copy-done((bf16[32,96,1024]{2,1,0:T(8,128)(2,1)S(1)}, bf16[32,96,1024]{2,1,0:T(8,128)(2,1)}, u32[]{:S(2)}) %copy-start) | copy-done | bytes 6291480
  7.6 34.2 %gather_blocks.1 = (bf16[4,256,1536]{2,1,0:T(8,128)(2,1)S(1)}, f32[8,8,128]{2,1,0:T(8,128)S(1)}) custom-call(s32[64]{0:T(128)S(1)} %reshape.10.orders_ref, bf16[32,96,1024]{2,1,0:T(8,128)(2,1)S(1)} %copy-done, bf16[32,32,1024]{2,1,0:T(8,128)(2,1)S(1)} %bitcast.2, f32[16,2,256]{2,1,0:T(2,128)S(1)} %copy-done.1), custom_call_target="tpu_custom_call" | custom-call | tf_op jit(solution)/shard_map/gather_blocks/pallas_call | solution.py:230
  41.8 3.8 %normal_maps.1 = (bf16[4,2,192,1536]{3,2,1,0:T(8,128)(2,1)}, f32[4,2,192]{2,1,0:T(2,128)}) custom-call(bf16[4,256,1536]{2,1,0:T(8,128)(2,1)S(1)} %get-tuple-element.4.blocks_ref, f32[8,8,128]{2,1,0:T(8,128)S(1)} %get-tuple-element.5.spectra_ref), custom_call_target="tpu_custom_call" | custom-call | tf_op jit(solution)/shard_map/normal_maps/pallas_call | solution.py:305
Async XLA Ops:
  0.6 4.2 %copy-start.1 = (f32[16,2,256]{2,1,0:T(2,128)S(1)}, f32[16,2,256]{2,1,0:T(2,128)}, u32[]{:S(2)}) copy-start(f32[16,2,256]{2,1,0:T(2,128)} %visibility_ref.1) | copy-start | bytes 98308
  4.8 2.8 %copy-start = (bf16[32,96,1024]{2,1,0:T(8,128)(2,1)S(1)}, bf16[32,96,1024]{2,1,0:T(8,128)(2,1)}, u32[]{:S(2)}) copy-start(bf16[32,96,1024]{2,1,0:T(8,128)(2,1)} %legendre_ref.1) | copy-start | bytes 18874372

commit v2 on v1

v2 whole, which is shorter than its diff:
```python
import functools
import math

import jax
import jax.numpy as jnp
from jax import lax
from jax.experimental import pallas as pl
from jax.experimental.pallas import tpu as pltpu
from jax.sharding import PartitionSpec as P

F32 = jnp.float32
BF16 = jnp.bfloat16
MESH = pl.DeviceIdType.MESH

NZ = 4
NY = 4
NX = 4
CAP = 4
ORDERS = 32
DEG = 96
PACK = 112
ROWS = 32
COLS = 1536
GROUP = 8
RELATIVE = (0, 1, 3, 2)


def gather_kernel(
    orders_ref, legendre_ref, beam_ref, visibility_ref,
    held, spectra,
    orders, legendre, beam, visibility, rows, products, harmonic, outgoing, arrived,
    load_sem, beam_sem, a_send, a_recv, x_send, x_recv, c_send, c_recv, s_send, s_recv,
):
    bl = lax.axis_index("bl")
    ma = lax.axis_index("ma")
    x, core = bl // 2, bl % 2
    z, y = ma // NY, ma % NY
    right = ((x + 1) % NX) * 2 + core
    left = ((x + NX - 1) % NX) * 2 + core
    across = ((x + 2) % NX) * 2 + core
    sibling = x * 2 + (1 - core)

    visibility_load = pltpu.make_async_copy(visibility_ref, visibility, beam_sem.at[0])
    visibility_load.start()
    beam_load = pltpu.make_async_copy(beam_ref, beam, beam_sem.at[1])
    beam_load.start()
    loads = []
    for g in range(ORDERS // GROUP):
        part = pl.ds(g * GROUP, GROUP)
        load = pltpu.make_async_copy(legendre_ref.at[part], legendre.at[part], load_sem.at[g])
        load.start()
        loads.append(load)
    orders_load = pltpu.make_async_copy(orders_ref, orders, beam_sem.at[2])
    orders_load.start()

    barrier = pltpu.get_barrier_semaphore()
    for d in range(1, NZ * NY):
        peer = ((z + d // NY) % NZ) * NY + (y + d) % NY
        pl.semaphore_signal(barrier, inc=1, device_id={"bl": bl, "ma": peer}, device_id_type=MESH)
    for d in range(1, 2 * NX):
        peer = (bl + d) % (2 * NX)
        pl.semaphore_signal(barrier, inc=1, device_id={"bl": peer, "ma": ma}, device_id_type=MESH)

    times = visibility_ref.shape[2]
    total_time = times * NZ * NY
    order_index = lax.broadcasted_iota(jnp.int32, (ORDERS, times), 0)
    time_index = lax.broadcasted_iota(jnp.int32, (ORDERS, times), 1) + ma * times
    angle = ((order_index * time_index) & (total_time - 1)).astype(F32) * (2.0 * math.pi / total_time)
    cosine, sine = jnp.cos(angle), jnp.sin(angle)
    visibility_load.wait()
    real = visibility[:, 0, :]
    imag = visibility[:, 1, :]
    direct = jnp.concatenate([real, imag] * CAP, axis=0)
    turned = jnp.concatenate([imag, -real] * CAP, axis=0)
    contract = (((1,), (1,)), ((), ()))
    partial = (
        lax.dot_general(cosine, direct, contract, precision=lax.Precision.HIGHEST, preferred_element_type=F32)
        + lax.dot_general(sine, turned, contract, precision=lax.Precision.HIGHEST, preferred_element_type=F32)
    ) * (1.0 / math.sqrt(total_time))
    high = partial.astype(BF16).astype(F32)
    low = partial - high
    row = lax.broadcasted_iota(jnp.int32, (PACK - DEG, 128), 0)
    for m in range(ORDERS):
        harmonic[m, DEG:PACK, :] = jnp.where(
            row == 0, high[m : m + 1], jnp.where(row == 1, low[m : m + 1], 0.0)
        ).astype(BF16)
    harmonic[ORDERS] = jnp.zeros((PACK, 128), BF16)

    beam_load.wait()
    for g in range(ORDERS // GROUP):
        rows[g] = beam[:, g * GROUP : (g + 1) * GROUP].reshape(GROUP * ROWS, -1)
    part = GROUP // 2
    for g in range(ORDERS // GROUP):
        loads[g].wait()
        for first in range(0, GROUP, part):
            product = lax.dot_general(
                legendre[g * GROUP + first : g * GROUP + first + part].reshape(part * DEG, -1),
                rows[g],
                contract,
                preferred_element_type=F32,
            ).astype(BF16)
            for i in range(part):
                products[first + i, g * DEG : (g + 1) * DEG] = product[i * DEG : (i + 1) * DEG]
    source = lax.broadcasted_iota(jnp.int32, (GROUP * ROWS, 128), 0)
    column = lax.broadcasted_iota(jnp.int32, (GROUP * ROWS, 128), 1) % ROWS
    wanted = (column % (ROWS // 2)) * (2 * GROUP) + column // (ROWS // 2)
    for i in range(GROUP):
        pick = (source == wanted + 2 * i).astype(F32).astype(BF16)
        picked = jnp.dot(products[i], pick, preferred_element_type=F32).astype(BF16)
        for g in range(ORDERS // GROUP):
            harmonic[g * GROUP + i, 0:DEG, :] = picked[g * DEG : (g + 1) * DEG]
    orders_load.wait()

    pl.semaphore_wait(barrier, NZ * NY - 1 + 2 * NX - 1)

    slot_lane = lax.broadcasted_iota(jnp.int32, (PACK, 128), 1) // ROWS
    def to_owner(t, dy):
        n = t * NY + dy
        owner = ((z + NZ - RELATIVE[t]) % NZ) * NY + (y + dy) % NY
        parts = [harmonic[orders[s, owner]] for s in range(CAP)]
        block = jnp.where(
            slot_lane < 2,
            jnp.where(slot_lane == 0, parts[0], parts[1]),
            jnp.where(slot_lane == 2, parts[2], parts[3]),
        )
        if n == 0:
            arrived[ma] = block
            return
        outgoing[n] = block
        copy = pltpu.make_async_remote_copy(
            src_ref=outgoing.at[n],
            dst_ref=arrived.at[ma],
            send_sem=a_send,
            recv_sem=a_recv.at[t],
            device_id={"bl": bl, "ma": owner},
            device_id_type=MESH,
        )
        copy.start()

    for t in range(NZ):
        for dy in range(NY):
            to_owner(t, dy)

    def view(t, who, first=0, count=CAP):
        return held.at[(z + RELATIVE[t]) % NZ, who, pl.ds(first, count)]

    def send(ref, to, send_sem, recv_sem):
        copy = pltpu.make_async_remote_copy(
            src_ref=ref, dst_ref=ref, send_sem=send_sem, recv_sem=recv_sem,
            device_id={"bl": to, "ma": ma}, device_id_type=MESH,
        )
        copy.start()

    def await_bytes(ref, sem):
        pltpu.make_async_copy(ref, ref, sem).wait()

    def own_part(t):
        zs = (z + RELATIVE[t]) % NZ
        count = NY if t else NY - 1
        await_bytes(arrived.at[pl.ds(0, count)], a_recv.at[t])
        stacked = jnp.concatenate([arrived[zs * NY + j, 0:DEG, :] for j in range(NY)], axis=0)
        held[zs, bl] = stacked.T.reshape(CAP, ROWS, NY * DEG)
        send(view(t, bl), right, x_send, x_recv.at[t, 0])
        send(view(t, bl), left, x_send, x_recv.at[t, 1])
        send(view(t, bl), sibling, c_send, c_recv)

    def near_part(t):
        await_bytes(view(t, left), x_recv.at[t, 0])
        send(view(t, left, 0, CAP // 2), right, x_send, x_recv.at[t, 2])
        send(view(t, left), sibling, c_send, c_recv)
        await_bytes(view(t, right), x_recv.at[t, 1])
        send(view(t, right, CAP // 2, CAP // 2), left, x_send, x_recv.at[t, 2])
        send(view(t, right), sibling, c_send, c_recv)

    def far_part(t):
        await_bytes(view(t, across), x_recv.at[t, 2])
        send(view(t, across), sibling, c_send, c_recv)

    own_part(0)
    own_part(1)
    near_part(0)
    own_part(2)
    own_part(3)

    total = jnp.zeros((PACK - DEG, 128), F32)
    for k in range(NZ * NY):
        total = total + arrived[k, DEG:PACK, :].astype(F32)
    line = jnp.sum(total, axis=0, keepdims=True).astype(BF16).astype(F32)
    spectra[bl] = jnp.broadcast_to(line, (8, 128))
    for d in range(1, 2 * NX):
        copy = pltpu.make_async_remote_copy(
            src_ref=spectra.at[bl], dst_ref=spectra.at[bl], send_sem=s_send, recv_sem=s_recv,
            device_id={"bl": (bl + d) % (2 * NX), "ma": ma}, device_id_type=MESH,
        )
        copy.start()

    near_part(1)
    far_part(0)
    near_part(2)
    far_part(1)
    near_part(3)
    far_part(2)
    far_part(3)

    await_bytes(held.at[pl.ds(0, NZ // 2)], c_recv)
    await_bytes(spectra.at[pl.ds(0, 2 * NX - 1)], s_recv)
    await_bytes(outgoing.at[pl.ds(0, NZ * NY - 1)], a_send)
    await_bytes(held.at[pl.ds(0, NZ - 1), pl.ds(0, NX)], x_send)
    await_bytes(held.at[pl.ds(0, NZ // 2)], c_send)
    await_bytes(spectra.at[pl.ds(0, 2 * NX - 1)], s_send)


def gather(orders, legendre, beam, visibility):
    hbm = pl.BlockSpec(memory_space=pltpu.HBM)
    vmem = pl.BlockSpec(memory_space=pltpu.VMEM)
    dma = pltpu.SemaphoreType.DMA
    return pl.pallas_call(
        gather_kernel,
        out_shape=(
            jax.ShapeDtypeStruct((NZ, 2 * NX, CAP, ROWS, NY * DEG), BF16),
            jax.ShapeDtypeStruct((2 * NX, 8, 128), F32),
        ),
        in_specs=[
            hbm,
            hbm,
            hbm,
            hbm,
        ],
        out_specs=(vmem, vmem),
        scratch_shapes=[
            pltpu.SMEM(orders.shape, jnp.int32),
            pltpu.VMEM(legendre.shape, BF16),
            pltpu.VMEM(beam.shape, BF16),
            pltpu.VMEM(visibility.shape, F32),
            pltpu.VMEM((ORDERS // GROUP, GROUP * ROWS, beam.shape[3]), BF16),
            pltpu.VMEM((GROUP, ORDERS // GROUP * DEG, GROUP * ROWS), BF16),
            pltpu.VMEM((ORDERS + 1, PACK, 128), BF16),
            pltpu.VMEM((NZ * NY, PACK, 128), BF16),
            pltpu.VMEM((NZ * NY, PACK, 128), BF16),
            dma((ORDERS // GROUP,)),
            dma((3,)),
            dma,
            dma((NZ,)),
            dma,
            dma((NZ, 3)),
            dma,
            dma,
            dma,
            dma,
        ],
        compiler_params=pltpu.CompilerParams(
            collective_id=0, has_side_effects=True, vmem_limit_bytes=40 * 1024 * 1024
        ),
        name="gather_blocks",
    )(orders, legendre, beam, visibility)


def normal_kernel(blocks_ref, spectra_ref, normal_ref, map_ref, turned, own):
    s = pl.program_id(0)
    bl = lax.axis_index("bl")
    start = pl.multiple_of((bl % 2) * 128, 128)
    skip = pl.multiple_of((bl % 2) * 64, 16)
    window = blocks_ref[bl // 2, :, s, :, pl.ds(start, 256)].reshape(2 * NX * ROWS, 256)
    pieces = []
    for k in range(2 * NX):
        pieces.append(-window[k * ROWS + ROWS // 2 : (k + 1) * ROWS])
        pieces.append(window[k * ROWS : k * ROWS + ROWS // 2])
    own[...] = window.T
    turned[...] = jnp.concatenate(pieces, axis=0).T
    left = jnp.concatenate([own[pl.ds(skip, 192), :], turned[pl.ds(skip, 192), :]], axis=0)
    scale = 1.0 / 128.0
    width = NY * DEG
    for n in range(0, NZ, 2):
        right = jnp.concatenate(
            [blocks_ref[n + h, :, s].reshape(2 * NX * ROWS, width) for h in range(2)], axis=1
        )
        product = jnp.dot(left, right, preferred_element_type=F32) * scale
        part = pl.ds(n * width, 2 * width)
        normal_ref[0, 0, :, part] = product[0:192].astype(BF16)
        normal_ref[0, 1, :, part] = product[192:384].astype(BF16)
    lane = lax.broadcasted_iota(jnp.int32, (8, 128), 1) // ROWS
    halves = []
    for h in range(2):
        line = jnp.zeros((8, 128), F32)
        for q in range(4):
            moved = pltpu.roll(spectra_ref[h * 4 + q], (q * ROWS + 128 - s * ROWS) % 128, 1)
            line = jnp.where(lane == q, moved, line)
        halves.append(line)
    spectrum = jnp.concatenate(halves, axis=1).astype(BF16)
    adjoint = lax.dot_general(spectrum, left, (((1,), (1,)), ((), ())), preferred_element_type=F32)
    adjoint = adjoint * (1.0 / math.sqrt(128.0))
    map_ref[0, 0:1, :] = adjoint[0:1, 0:192]
    map_ref[0, 1:2, :] = adjoint[0:1, 192:384]


def normal_maps(blocks, spectra):
    return pl.pallas_call(
        normal_kernel,
        grid=(CAP,),
        out_shape=(
            jax.ShapeDtypeStruct((CAP, 2, 192, COLS), BF16),
            jax.ShapeDtypeStruct((CAP, 2, 192), F32),
        ),
        in_specs=[
            pl.BlockSpec(memory_space=pltpu.VMEM),
            pl.BlockSpec(memory_space=pltpu.VMEM),
        ],
        out_specs=(
            pl.BlockSpec((1, 2, 192, COLS), lambda s: (s, 0, 0, 0)),
            pl.BlockSpec((1, 2, 192), lambda s: (s, 0, 0)),
        ),
        scratch_shapes=[pltpu.VMEM((256, 256), BF16), pltpu.VMEM((256, 256), BF16)],
        compiler_params=pltpu.CompilerParams(vmem_limit_bytes=40 * 1024 * 1024),
        name="normal_maps",
    )(blocks, spectra)


def on_device(beam_fringe_harmonics, legendre, visibility, owner_orders):
    in_hbm = [
        pltpu.with_memory_space_constraint(a, pltpu.HBM)
        for a in (owner_orders.T, legendre, beam_fringe_harmonics, visibility)
    ]
    blocks, spectra = gather(*in_hbm)
    return normal_maps(blocks, spectra)


def solution(mesh):
    return jax.shard_map(
        on_device,
        mesh=mesh,
        in_specs=(P("bl", None, None, None), P(None, "ma", None), P("bl", None, "ma"), P()),
        out_specs=(P("ma", None, "bl", None), P("ma", None, "bl")),
        check_vma=False,
    )
```

time: 45.8 us -> 36.7 us (0.80)
  local copies, waits for them, and re-layouts: 6.95 us -> 0 us
  Pallas kernels: 37.9 us -> 36 us
    unnamed x5 -> x0, local copies, waits for them, and re-layouts: 3.55 us -> none
    transpose x1 -> x0, local copies, waits for them, and re-layouts: 3.32 us -> none  [on_device(): beam = beam_fringe_harmonics.transpose(1, 2, 0, 3).reshape(ORDERS, ROWS, -1)]
    pallas_call x1, Pallas kernels: 34.2 us -> 32.2 us  [gather(): pl.pallas_call(gather_kernel, out_shape=(jax.ShapeDtypeStruct((NZ, 2 * NX...]
where the time goes in v2:
time: 36.7 us; the launch traced here: 36.6 us
  Pallas kernels  36 us (98%)
  between operations  0.64 us (2%)
    pallas_call x1, Pallas kernels, gather(): pl.pallas_call(gather_kernel, out_shape=(jax.ShapeDtypeStruct((NZ, 2 * NX...  32.2 us
    pallas_call x1, Pallas kernels, normal_maps(): pl.pallas_call(normal_kernel, grid=(CAP,), out_shape=(jax.ShapeDtypeStruc...  3.78 us

profile of v2, /device:TPU:1, one launch (start us, length us, event | category | flops | bytes accessed | tf_op | source)
XLA Modules:
  0.0 36.6 jit_solution(3260483900278173337)
XLA Ops:
  0.6 32.2 %gather_blocks.1 = (bf16[4,8,4,32,384]{4,3,2,1,0:T(8,128)(2,1)S(1)}, f32[8,8,128]{2,1,0:T(8,128)S(1)}) custom-call(s32[4,16]{1,0:T(4,128)} %bitcast.1, bf16[32,96,1024]{2,1,0:T(8,128)(2,1)} %legendre_ref.1, bf16[16,32,2,1024]{3,2,1,0:T(2,128)(2,1)} %beam_ref.1, f32[16,2,256]{2,1,0:T(2,128)} %visibility_ref.1), custom_call_target="tpu_custom_call" | custom-call | tf_op jit(solution)/shard_map/gather_blocks/pallas_call | solution.py:217
  32.8 3.8 %normal_maps.1 = (bf16[4,2,192,1536]{3,2,1,0:T(8,128)(2,1)}, f32[4,2,192]{2,1,0:T(2,128)}) custom-call(bf16[4,8,4,32,384]{4,3,2,1,0:T(8,128)(2,1)S(1)} %get-tuple-element.4.blocks_ref, f32[8,8,128]{2,1,0:T(8,128)S(1)} %get-tuple-element.5.spectra_ref), custom_call_target="tpu_custom_call" | custom-call | tf_op jit(solution)/shard_map/normal_maps/pallas_call | solution.py:297

commit v3 on v2

--- a/solution.py
+++ b/solution.py
@@ -22,14 +22,15 @@
 ROWS = 32
 COLS = 1536
 GROUP = 8
-RELATIVE = (0, 1, 3, 2)
 
 
 def gather_kernel(
     orders_ref, legendre_ref, beam_ref, visibility_ref,
     held, spectra,
     orders, legendre, beam, visibility, rows, products, harmonic, outgoing, arrived,
-    load_sem, beam_sem, a_send, a_recv, x_send, x_recv, c_send, c_recv, s_send, s_recv,
+    crossed, lined,
+    load_sem, beam_sem, a_send, a_recv, k_send, k_recv, l_send, l_recv, p_send, p_recv,
+    x_send, x_recv, c_send, c_recv, s_send, s_recv,
 ):
     bl = lax.axis_index("bl")
     ma = lax.axis_index("ma")
@@ -113,99 +114,164 @@
 
     pl.semaphore_wait(barrier, NZ * NY - 1 + 2 * NX - 1)
 
+    def row(t, at_y):
+        sign = 1 - 2 * (at_y % 2)
+        return (0, sign, -sign, 2)[t]
+
+    def owner_at(t, dy):
+        at_y = (y + dy) % NY
+        return (z + NZ - row(t, at_y)) % NZ, at_y
+
     slot_lane = lax.broadcasted_iota(jnp.int32, (PACK, 128), 1) // ROWS
-    def to_owner(t, dy):
-        n = t * NY + dy
-        owner = ((z + NZ - RELATIVE[t]) % NZ) * NY + (y + dy) % NY
+
+    def block_for(at_z, at_y):
+        owner = at_z * NY + at_y
         parts = [harmonic[orders[s, owner]] for s in range(CAP)]
-        block = jnp.where(
+        return jnp.where(
             slot_lane < 2,
             jnp.where(slot_lane == 0, parts[0], parts[1]),
             jnp.where(slot_lane == 2, parts[2], parts[3]),
         )
-        if n == 0:
-            arrived[ma] = block
-            return
-        outgoing[n] = block
-        copy = pltpu.make_async_remote_copy(
-            src_ref=outgoing.at[n],
-            dst_ref=arrived.at[ma],
-            send_sem=a_send,
-            recv_sem=a_recv.at[t],
-            device_id={"bl": bl, "ma": owner},
-            device_id_type=MESH,
-        )
-        copy.start()
-
-    for t in range(NZ):
-        for dy in range(NY):
-            to_owner(t, dy)
-
-    def view(t, who, first=0, count=CAP):
-        return held.at[(z + RELATIVE[t]) % NZ, who, pl.ds(first, count)]
-
-    def send(ref, to, send_sem, recv_sem):
-        copy = pltpu.make_async_remote_copy(
-            src_ref=ref, dst_ref=ref, send_sem=send_sem, recv_sem=recv_sem,
-            device_id={"bl": to, "ma": ma}, device_id_type=MESH,
-        )
-        copy.start()
+
+    def send(source, target, send_sem, recv_sem, to_bl, to_ma):
+        pltpu.make_async_remote_copy(
+            src_ref=source, dst_ref=target, send_sem=send_sem, recv_sem=recv_sem,
+            device_id={"bl": to_bl, "ma": to_ma}, device_id_type=MESH,
+        ).start()
 
     def await_bytes(ref, sem):
         pltpu.make_async_copy(ref, ref, sem).wait()
 
+    for t in (1, 0):
+        for dy in range(NY):
+            at_z, at_y = owner_at(t, dy)
+            block = block_for(at_z, at_y)
+            crossed[x, t, at_y] = block[0:DEG]
+            if t or dy:
+                outgoing[t * NY + dy, DEG:PACK] = block[DEG:PACK]
+            else:
+                arrived[ma, DEG:PACK] = block[DEG:PACK]
+        ref = crossed.at[x, t]
+        send(ref, ref, k_send, k_recv.at[t, 0], right, ma)
+        send(ref, ref, k_send, k_recv.at[t, 1], left, ma)
+
+    for t in (2, 3):
+        for dy in range(NY):
+            at_z, at_y = owner_at(t, dy)
+            n = t * NY + dy
+            outgoing[n] = block_for(at_z, at_y)
+            send(outgoing.at[n], arrived.at[ma], a_send, a_recv.at[t - 2], bl, at_z * NY + at_y)
+
+    def pass_on(t, n, who):
+        for dy in range(NY):
+            if t or dy:
+                at_z, at_y = owner_at(t, dy)
+                send(crossed.at[who // 2, t, at_y], lined.at[t, who // 2, y],
+                     l_send.at[t], l_recv.at[t, n], bl, at_z * NY + at_y)
+
+    pass_on(1, 0, bl)
+    pass_on(0, 0, bl)
+    for t in (1, 0):
+        for dy in range(NY):
+            if t or dy:
+                at_z, at_y = owner_at(t, dy)
+                send(outgoing.at[t * NY + dy, pl.ds(DEG, PACK - DEG)], arrived.at[ma, pl.ds(DEG, PACK - DEG)],
+                     p_send, p_recv, bl, at_z * NY + at_y)
+
+    def cross_near(t):
+        ref = crossed.at[left // 2, t]
+        await_bytes(ref, k_recv.at[t, 0])
+        half = crossed.at[left // 2, t, pl.ds(0, NY // 2)]
+        send(half, half, k_send, k_recv.at[t, 2], right, ma)
+        pass_on(t, 1, left)
+        ref = crossed.at[right // 2, t]
+        await_bytes(ref, k_recv.at[t, 1])
+        half = crossed.at[right // 2, t, pl.ds(NY // 2, NY // 2)]
+        send(half, half, k_send, k_recv.at[t, 2], left, ma)
+        pass_on(t, 2, right)
+
+    def cross_far(t):
+        await_bytes(crossed.at[across // 2, t], k_recv.at[t, 2])
+        pass_on(t, 3, across)
+
+    def view(t, who, first=0, count=CAP):
+        return held.at[(z + NZ + row(t, y)) % NZ, who, pl.ds(first, count)]
+
+    def to_sibling(t, who):
+        ref = view(t, who)
+        send(ref, ref, c_send, c_recv, sibling, ma)
+
+    def keep(t, who, blocks):
+        stacked = jnp.concatenate(blocks, axis=0)
+        held[(z + NZ + row(t, y)) % NZ, who] = stacked.T.reshape(CAP, ROWS, NY * DEG)
+
+    def collect(t, n, who):
+        await_bytes(lined.at[t, 0, pl.ds(0, NY if t else NY - 1)], l_recv.at[t, n])
+        if t == 0:
+            lined[t, who // 2, y] = crossed[who // 2, t, y]
+        keep(t, who, [lined[t, who // 2, j] for j in range(NY)])
+        to_sibling(t, who)
+
     def own_part(t):
-        zs = (z + RELATIVE[t]) % NZ
-        count = NY if t else NY - 1
-        await_bytes(arrived.at[pl.ds(0, count)], a_recv.at[t])
-        stacked = jnp.concatenate([arrived[zs * NY + j, 0:DEG, :] for j in range(NY)], axis=0)
-        held[zs, bl] = stacked.T.reshape(CAP, ROWS, NY * DEG)
-        send(view(t, bl), right, x_send, x_recv.at[t, 0])
-        send(view(t, bl), left, x_send, x_recv.at[t, 1])
-        send(view(t, bl), sibling, c_send, c_recv)
+        await_bytes(arrived.at[pl.ds(0, NY)], a_recv.at[t - 2])
+        at_z = (z + NZ + row(t, y)) % NZ
+        keep(t, bl, [arrived[at_z * NY + j, 0:DEG, :] for j in range(NY)])
+        ref = view(t, bl)
+        send(ref, ref, x_send, x_recv.at[t - 2, 0], right, ma)
+        send(ref, ref, x_send, x_recv.at[t - 2, 1], left, ma)
+        to_sibling(t, bl)
 
     def near_part(t):
-        await_bytes(view(t, left), x_recv.at[t, 0])
-        send(view(t, left, 0, CAP // 2), right, x_send, x_recv.at[t, 2])
-        send(view(t, left), sibling, c_send, c_recv)
-        await_bytes(view(t, right), x_recv.at[t, 1])
-        send(view(t, right, CAP // 2, CAP // 2), left, x_send, x_recv.at[t, 2])
-        send(view(t, right), sibling, c_send, c_recv)
+        await_bytes(view(t, left), x_recv.at[t - 2, 0])
+        ref = view(t, left, 0, CAP // 2)
+        send(ref, ref, x_send, x_recv.at[t - 2, 2], right, ma)
+        to_sibling(t, left)
+        await_bytes(view(t, right), x_recv.at[t - 2, 1])
+        ref = view(t, right, CAP // 2, CAP // 2)
+        send(ref, ref, x_send, x_recv.at[t - 2, 2], left, ma)
+        to_sibling(t, right)
 
     def far_part(t):
-        await_bytes(view(t, across), x_recv.at[t, 2])
-        send(view(t, across), sibling, c_send, c_recv)
-
-    own_part(0)
-    own_part(1)
-    near_part(0)
+        await_bytes(view(t, across), x_recv.at[t - 2, 2])
+        to_sibling(t, across)
+
+    cross_near(1)
+    cross_near(0)
     own_part(2)
     own_part(3)
-
+    cross_far(1)
+    cross_far(0)
+    collect(1, 0, bl)
+    collect(0, 0, bl)
+
+    await_bytes(arrived.at[pl.ds(0, 2 * NY - 1), pl.ds(DEG, PACK - DEG)], p_recv)
     total = jnp.zeros((PACK - DEG, 128), F32)
     for k in range(NZ * NY):
         total = total + arrived[k, DEG:PACK, :].astype(F32)
     line = jnp.sum(total, axis=0, keepdims=True).astype(BF16).astype(F32)
     spectra[bl] = jnp.broadcast_to(line, (8, 128))
     for d in range(1, 2 * NX):
-        copy = pltpu.make_async_remote_copy(
-            src_ref=spectra.at[bl], dst_ref=spectra.at[bl], send_sem=s_send, recv_sem=s_recv,
-            device_id={"bl": (bl + d) % (2 * NX), "ma": ma}, device_id_type=MESH,
-        )
-        copy.start()
-
-    near_part(1)
-    far_part(0)
+        send(spectra.at[bl], spectra.at[bl], s_send, s_recv, (bl + d) % (2 * NX), ma)
+
+    collect(1, 1, left)
+    collect(1, 2, right)
+    collect(0, 1, left)
+    collect(0, 2, right)
     near_part(2)
-    far_part(1)
     near_part(3)
+    collect(1, 3, across)
+    collect(0, 3, across)
     far_part(2)
     far_part(3)
 
     await_bytes(held.at[pl.ds(0, NZ // 2)], c_recv)
     await_bytes(spectra.at[pl.ds(0, 2 * NX - 1)], s_recv)
-    await_bytes(outgoing.at[pl.ds(0, NZ * NY - 1)], a_send)
-    await_bytes(held.at[pl.ds(0, NZ - 1), pl.ds(0, NX)], x_send)
+    await_bytes(crossed.at[pl.ds(0, NX - 1)], k_send)
+    await_bytes(outgoing.at[pl.ds(0, 2 * NY)], a_send)
+    await_bytes(outgoing.at[pl.ds(0, 2 * NY - 1), pl.ds(DEG, PACK - DEG)], p_send)
+    await_bytes(crossed.at[pl.ds(0, NX - 1), 0], l_send.at[0])
+    await_bytes(crossed.at[:, 1], l_send.at[1])
+    await_bytes(held.at[0, pl.ds(0, NX + 2)], x_send)
     await_bytes(held.at[pl.ds(0, NZ // 2)], c_send)
     await_bytes(spectra.at[pl.ds(0, 2 * NX - 1)], s_send)
 
@@ -237,12 +303,20 @@
             pltpu.VMEM((ORDERS + 1, PACK, 128), BF16),
             pltpu.VMEM((NZ * NY, PACK, 128), BF16),
             pltpu.VMEM((NZ * NY, PACK, 128), BF16),
+            pltpu.VMEM((NX, 2, NY, DEG, 128), BF16),
+            pltpu.VMEM((2, NX, NY, DEG, 128), BF16),
             dma((ORDERS // GROUP,)),
             dma((3,)),
             dma,
-            dma((NZ,)),
-            dma,
-            dma((NZ, 3)),
+            dma((2,)),
+            dma,
+            dma((2, 3)),
+            dma((2,)),
+            dma((2, 4)),
+            dma,
+            dma,
+            dma,
+            dma((2, 3)),
             dma,
             dma,
             dma,

time: 36.7 us -> 33.4 us (0.910)
  the two profiles are of different devices: /device:TPU:1 before, /device:TPU:17 now
where the time goes in v3:
time: 33.4 us; the launch traced here: 33.3 us
  Pallas kernels  32.7 us (98%)
  between operations  0.64 us (2%)
    pallas_call x1, Pallas kernels, gather(): pl.pallas_call(gather_kernel, out_shape=(jax.ShapeDtypeStruct((NZ, 2 * NX...  28.9 us
    pallas_call x1, Pallas kernels, normal_maps(): pl.pallas_call(normal_kernel, grid=(CAP,), out_shape=(jax.ShapeDtypeStruc...  3.78 us

profile of v3, /device:TPU:17, one launch (start us, length us, event | category | flops | bytes accessed | tf_op | source)
XLA Modules:
  0.0 33.3 jit_solution(10819400291699400730)
XLA Ops:
  0.6 28.9 %gather_blocks.1 = (bf16[4,8,4,32,384]{4,3,2,1,0:T(8,128)(2,1)S(1)}, f32[8,8,128]{2,1,0:T(8,128)S(1)}) custom-call(s32[4,16]{1,0:T(4,128)} %bitcast.1, bf16[32,96,1024]{2,1,0:T(8,128)(2,1)} %legendre_ref.1, bf16[16,32,2,1024]{3,2,1,0:T(2,128)(2,1)} %beam_ref.1, f32[16,2,256]{2,1,0:T(2,128)} %visibility_ref.1), custom_call_target="tpu_custom_call" | custom-call | tf_op jit(solution)/shard_map/gather_blocks/pallas_call | solution.py:283
  29.5 3.8 %normal_maps.1 = (bf16[4,2,192,1536]{3,2,1,0:T(8,128)(2,1)}, f32[4,2,192]{2,1,0:T(2,128)}) custom-call(bf16[4,8,4,32,384]{4,3,2,1,0:T(8,128)(2,1)S(1)} %get-tuple-element.4.blocks_ref, f32[8,8,128]{2,1,0:T(8,128)S(1)} %get-tuple-element.5.spectra_ref), custom_call_target="tpu_custom_call" | custom-call | tf_op jit(solution)/shard_map/normal_maps/pallas_call | solution.py:371

commit v4 on v3

--- a/solution.py
+++ b/solution.py
@@ -27,9 +27,9 @@
 def gather_kernel(
     orders_ref, legendre_ref, beam_ref, visibility_ref,
     held, spectra,
-    orders, legendre, beam, visibility, rows, products, harmonic, outgoing, arrived,
+    orders, legendre, beam, visibility, products, harmonic, outgoing, arrived,
     crossed, lined,
-    load_sem, beam_sem, a_send, a_recv, k_send, k_recv, l_send, l_recv, p_send, p_recv,
+    legendre_sem, beam_sem, small_sem, a_send, a_recv, k_send, k_recv, l_send, l_recv, p_send, p_recv,
     x_send, x_recv, c_send, c_recv, s_send, s_recv,
 ):
     bl = lax.axis_index("bl")
@@ -41,17 +41,19 @@
     across = ((x + 2) % NX) * 2 + core
     sibling = x * 2 + (1 - core)
 
-    visibility_load = pltpu.make_async_copy(visibility_ref, visibility, beam_sem.at[0])
+    visibility_load = pltpu.make_async_copy(visibility_ref, visibility, small_sem.at[0])
     visibility_load.start()
-    beam_load = pltpu.make_async_copy(beam_ref, beam, beam_sem.at[1])
-    beam_load.start()
     loads = []
     for g in range(ORDERS // GROUP):
         part = pl.ds(g * GROUP, GROUP)
-        load = pltpu.make_async_copy(legendre_ref.at[part], legendre.at[part], load_sem.at[g])
-        load.start()
-        loads.append(load)
-    orders_load = pltpu.make_async_copy(orders_ref, orders, beam_sem.at[2])
+        pair = (
+            pltpu.make_async_copy(beam_ref.at[:, part], beam.at[:, part], beam_sem.at[g]),
+            pltpu.make_async_copy(legendre_ref.at[part], legendre.at[part], legendre_sem.at[g]),
+        )
+        for load in pair:
+            load.start()
+        loads.append(pair)
+    orders_load = pltpu.make_async_copy(orders_ref, orders, small_sem.at[1])
     orders_load.start()
 
     barrier = pltpu.get_barrier_semaphore()
@@ -87,16 +89,14 @@
         ).astype(BF16)
     harmonic[ORDERS] = jnp.zeros((PACK, 128), BF16)
 
-    beam_load.wait()
-    for g in range(ORDERS // GROUP):
-        rows[g] = beam[:, g * GROUP : (g + 1) * GROUP].reshape(GROUP * ROWS, -1)
     part = GROUP // 2
     for g in range(ORDERS // GROUP):
-        loads[g].wait()
+        for load in loads[g]:
+            load.wait()
         for first in range(0, GROUP, part):
             product = lax.dot_general(
                 legendre[g * GROUP + first : g * GROUP + first + part].reshape(part * DEG, -1),
-                rows[g],
+                beam[:, g * GROUP : (g + 1) * GROUP].reshape(GROUP * ROWS, -1),
                 contract,
                 preferred_element_type=F32,
             ).astype(BF16)
@@ -151,9 +151,11 @@
                 outgoing[t * NY + dy, DEG:PACK] = block[DEG:PACK]
             else:
                 arrived[ma, DEG:PACK] = block[DEG:PACK]
-        ref = crossed.at[x, t]
-        send(ref, ref, k_send, k_recv.at[t, 0], right, ma)
-        send(ref, ref, k_send, k_recv.at[t, 1], left, ma)
+        lower, upper = (crossed.at[x, t, pl.ds(h * (NY // 2), NY // 2)] for h in range(2))
+        send(lower, lower, k_send, k_recv.at[t, 0], right, ma)
+        send(upper, upper, k_send, k_recv.at[t, 1], left, ma)
+        send(upper, upper, k_send, k_recv.at[t, 3], right, ma)
+        send(lower, lower, k_send, k_recv.at[t, 4], left, ma)
 
     for t in (2, 3):
         for dy in range(NY):
@@ -179,15 +181,15 @@
                      p_send, p_recv, bl, at_z * NY + at_y)
 
     def cross_near(t):
-        ref = crossed.at[left // 2, t]
-        await_bytes(ref, k_recv.at[t, 0])
         half = crossed.at[left // 2, t, pl.ds(0, NY // 2)]
+        await_bytes(half, k_recv.at[t, 0])
         send(half, half, k_send, k_recv.at[t, 2], right, ma)
+        half = crossed.at[right // 2, t, pl.ds(NY // 2, NY // 2)]
+        await_bytes(half, k_recv.at[t, 1])
+        send(half, half, k_send, k_recv.at[t, 2], left, ma)
+        await_bytes(half, k_recv.at[t, 3])
         pass_on(t, 1, left)
-        ref = crossed.at[right // 2, t]
-        await_bytes(ref, k_recv.at[t, 1])
-        half = crossed.at[right // 2, t, pl.ds(NY // 2, NY // 2)]
-        send(half, half, k_send, k_recv.at[t, 2], left, ma)
+        await_bytes(half, k_recv.at[t, 4])
         pass_on(t, 2, right)
 
     def cross_far(t):
@@ -216,19 +218,23 @@
         await_bytes(arrived.at[pl.ds(0, NY)], a_recv.at[t - 2])
         at_z = (z + NZ + row(t, y)) % NZ
         keep(t, bl, [arrived[at_z * NY + j, 0:DEG, :] for j in range(NY)])
-        ref = view(t, bl)
-        send(ref, ref, x_send, x_recv.at[t - 2, 0], right, ma)
-        send(ref, ref, x_send, x_recv.at[t - 2, 1], left, ma)
+        lower, upper = (view(t, bl, h * (CAP // 2), CAP // 2) for h in range(2))
+        send(lower, lower, x_send, x_recv.at[t - 2, 0], right, ma)
+        send(upper, upper, x_send, x_recv.at[t - 2, 1], left, ma)
+        send(upper, upper, x_send, x_recv.at[t - 2, 3], right, ma)
+        send(lower, lower, x_send, x_recv.at[t - 2, 4], left, ma)
         to_sibling(t, bl)
 
     def near_part(t):
-        await_bytes(view(t, left), x_recv.at[t - 2, 0])
-        ref = view(t, left, 0, CAP // 2)
-        send(ref, ref, x_send, x_recv.at[t - 2, 2], right, ma)
+        half = view(t, left, 0, CAP // 2)
+        await_bytes(half, x_recv.at[t - 2, 0])
+        send(half, half, x_send, x_recv.at[t - 2, 2], right, ma)
+        half = view(t, right, CAP // 2, CAP // 2)
+        await_bytes(half, x_recv.at[t - 2, 1])
+        send(half, half, x_send, x_recv.at[t - 2, 2], left, ma)
+        await_bytes(half, x_recv.at[t - 2, 3])
         to_sibling(t, left)
-        await_bytes(view(t, right), x_recv.at[t - 2, 1])
-        ref = view(t, right, CAP // 2, CAP // 2)
-        send(ref, ref, x_send, x_recv.at[t - 2, 2], left, ma)
+        await_bytes(half, x_recv.at[t - 2, 4])
         to_sibling(t, right)
 
     def far_part(t):
@@ -298,7 +304,6 @@
             pltpu.VMEM(legendre.shape, BF16),
             pltpu.VMEM(beam.shape, BF16),
             pltpu.VMEM(visibility.shape, F32),
-            pltpu.VMEM((ORDERS // GROUP, GROUP * ROWS, beam.shape[3]), BF16),
             pltpu.VMEM((GROUP, ORDERS // GROUP * DEG, GROUP * ROWS), BF16),
             pltpu.VMEM((ORDERS + 1, PACK, 128), BF16),
             pltpu.VMEM((NZ * NY, PACK, 128), BF16),
@@ -306,17 +311,18 @@
             pltpu.VMEM((NX, 2, NY, DEG, 128), BF16),
             pltpu.VMEM((2, NX, NY, DEG, 128), BF16),
             dma((ORDERS // GROUP,)),
-            dma((3,)),
-            dma,
+            dma((ORDERS // GROUP,)),
             dma((2,)),
             dma,
-            dma((2, 3)),
+            dma((2,)),
+            dma,
+            dma((2, 5)),
             dma((2,)),
             dma((2, 4)),
             dma,
             dma,
             dma,
-            dma((2, 3)),
+            dma((2, 5)),
             dma,
             dma,
             dma,
@@ -329,61 +335,79 @@
     )(orders, legendre, beam, visibility)
 
 
-def normal_kernel(blocks_ref, spectra_ref, normal_ref, map_ref, turned, own):
-    s = pl.program_id(0)
+def normal_kernel(blocks_ref, spectra_ref, normal_ref, map_ref, own, turned, result, maps, out_sem):
     bl = lax.axis_index("bl")
     start = pl.multiple_of((bl % 2) * 128, 128)
     skip = pl.multiple_of((bl % 2) * 64, 16)
-    window = blocks_ref[bl // 2, :, s, :, pl.ds(start, 256)].reshape(2 * NX * ROWS, 256)
-    pieces = []
-    for k in range(2 * NX):
-        pieces.append(-window[k * ROWS + ROWS // 2 : (k + 1) * ROWS])
-        pieces.append(window[k * ROWS : k * ROWS + ROWS // 2])
-    own[...] = window.T
-    turned[...] = jnp.concatenate(pieces, axis=0).T
-    left = jnp.concatenate([own[pl.ds(skip, 192), :], turned[pl.ds(skip, 192), :]], axis=0)
     scale = 1.0 / 128.0
     width = NY * DEG
-    for n in range(0, NZ, 2):
-        right = jnp.concatenate(
-            [blocks_ref[n + h, :, s].reshape(2 * NX * ROWS, width) for h in range(2)], axis=1
-        )
-        product = jnp.dot(left, right, preferred_element_type=F32) * scale
-        part = pl.ds(n * width, 2 * width)
-        normal_ref[0, 0, :, part] = product[0:192].astype(BF16)
-        normal_ref[0, 1, :, part] = product[192:384].astype(BF16)
+    copies = []
+
+    def prepare(s):
+        window = blocks_ref[bl // 2, :, s, :, pl.ds(start, 256)].reshape(2 * NX * ROWS, 256)
+        pieces = []
+        for k in range(2 * NX):
+            pieces.append(-window[k * ROWS + ROWS // 2 : (k + 1) * ROWS])
+            pieces.append(window[k * ROWS : k * ROWS + ROWS // 2])
+        own[s] = window.T
+        turned[s] = jnp.concatenate(pieces, axis=0).T
+
+    for s in range(CAP):
+        prepare(s)
+        left = jnp.concatenate([own[s, pl.ds(skip, 192), :], turned[s, pl.ds(skip, 192), :]], axis=0)
+        for n in range(0, NZ, 2):
+            right = jnp.concatenate(
+                [blocks_ref[n + h, :, s].reshape(2 * NX * ROWS, width) for h in range(2)], axis=1
+            )
+            product = jnp.dot(left, right, preferred_element_type=F32) * scale
+            part = pl.ds(n * width, 2 * width)
+            result[s, 0, :, part] = product[0:192].astype(BF16)
+            result[s, 1, :, part] = product[192:384].astype(BF16)
+            copy = pltpu.make_async_copy(
+                result.at[s, :, :, part], normal_ref.at[s, :, :, part], out_sem.at[s * (NZ // 2) + n // 2]
+            )
+            copy.start()
+            copies.append(copy)
     lane = lax.broadcasted_iota(jnp.int32, (8, 128), 1) // ROWS
-    halves = []
-    for h in range(2):
-        line = jnp.zeros((8, 128), F32)
-        for q in range(4):
-            moved = pltpu.roll(spectra_ref[h * 4 + q], (q * ROWS + 128 - s * ROWS) % 128, 1)
-            line = jnp.where(lane == q, moved, line)
-        halves.append(line)
-    spectrum = jnp.concatenate(halves, axis=1).astype(BF16)
-    adjoint = lax.dot_general(spectrum, left, (((1,), (1,)), ((), ())), preferred_element_type=F32)
-    adjoint = adjoint * (1.0 / math.sqrt(128.0))
-    map_ref[0, 0:1, :] = adjoint[0:1, 0:192]
-    map_ref[0, 1:2, :] = adjoint[0:1, 192:384]
+    for s in range(CAP):
+        left = jnp.concatenate([own[s, pl.ds(skip, 192), :], turned[s, pl.ds(skip, 192), :]], axis=0)
+        halves = []
+        for h in range(2):
+            line = jnp.zeros((8, 128), F32)
+            for q in range(4):
+                moved = pltpu.roll(spectra_ref[h * 4 + q], (q * ROWS + 128 - s * ROWS) % 128, 1)
+                line = jnp.where(lane == q, moved, line)
+            halves.append(line)
+        spectrum = jnp.concatenate(halves, axis=1).astype(BF16)
+        adjoint = lax.dot_general(spectrum, left, (((1,), (1,)), ((), ())), preferred_element_type=F32)
+        adjoint = adjoint * (1.0 / math.sqrt(128.0))
+        maps[s, 0:1, :] = adjoint[0:1, 0:192]
+        maps[s, 1:2, :] = adjoint[0:1, 192:384]
+    copy = pltpu.make_async_copy(maps, map_ref, out_sem.at[CAP * NZ // 2])
+    copy.start()
+    copies.append(copy)
+    for copy in copies:
+        copy.wait()
 
 
 def normal_maps(blocks, spectra):
+    hbm = pl.BlockSpec(memory_space=pltpu.HBM)
+    vmem = pl.BlockSpec(memory_space=pltpu.VMEM)
     return pl.pallas_call(
         normal_kernel,
-        grid=(CAP,),
         out_shape=(
             jax.ShapeDtypeStruct((CAP, 2, 192, COLS), BF16),
             jax.ShapeDtypeStruct((CAP, 2, 192), F32),
         ),
-        in_specs=[
-            pl.BlockSpec(memory_space=pltpu.VMEM),
-            pl.BlockSpec(memory_space=pltpu.VMEM),
+        in_specs=[vmem, vmem],
+        out_specs=(hbm, hbm),
+        scratch_shapes=[
+            pltpu.VMEM((CAP, 256, 256), BF16),
+            pltpu.VMEM((CAP, 256, 256), BF16),
+            pltpu.VMEM((CAP, 2, 192, COLS), BF16),
+            pltpu.VMEM((CAP, 2, 192), F32),
+            pltpu.SemaphoreType.DMA((CAP * NZ // 2 + 1,)),
         ],
-        out_specs=(
-            pl.BlockSpec((1, 2, 192, COLS), lambda s: (s, 0, 0, 0)),
-            pl.BlockSpec((1, 2, 192), lambda s: (s, 0, 0)),
-        ),
-        scratch_shapes=[pltpu.VMEM((256, 256), BF16), pltpu.VMEM((256, 256), BF16)],
         compiler_params=pltpu.CompilerParams(vmem_limit_bytes=40 * 1024 * 1024),
         name="normal_maps",
     )(blocks, spectra)

time: 33.4 us -> 32.1 us (0.961)
  the two profiles are of different devices: /device:TPU:17 before, /device:TPU:25 now
where the time goes in v4:
time: 32.1 us; the launch traced here: 32 us
  Pallas kernels  31.3 us (98%)
  between operations  0.64 us (2%)
    pallas_call x1, Pallas kernels, gather(): pl.pallas_call(gather_kernel, out_shape=(jax.ShapeDtypeStruct((NZ, 2 * NX...  28.6 us
    pallas_call x1, Pallas kernels, normal_maps(): pl.pallas_call(normal_kernel, out_shape=(jax.ShapeDtypeStruct((CAP, 2, 19...  2.71 us

profile of v4, /device:TPU:25, one launch (start us, length us, event | category | flops | bytes accessed | tf_op | source)
XLA Modules:
  0.0 32.0 jit_solution(12780971182733762330)
XLA Ops:
  0.6 28.6 %gather_blocks.1 = (bf16[4,8,4,32,384]{4,3,2,1,0:T(8,128)(2,1)S(1)}, f32[8,8,128]{2,1,0:T(8,128)S(1)}) custom-call(s32[4,16]{1,0:T(4,128)} %bitcast.1, bf16[32,96,1024]{2,1,0:T(8,128)(2,1)} %legendre_ref.1, bf16[16,32,2,1024]{3,2,1,0:T(2,128)(2,1)} %beam_ref.1, f32[16,2,256]{2,1,0:T(2,128)} %visibility_ref.1), custom_call_target="tpu_custom_call" | custom-call | tf_op jit(solution)/shard_map/gather_blocks/pallas_call | solution.py:289
  29.2 2.7 %normal_maps.1 = (bf16[4,2,192,1536]{3,2,1,0:T(8,128)(2,1)}, f32[4,2,192]{2,1,0:T(2,128)}) custom-call(bf16[4,8,4,32,384]{4,3,2,1,0:T(8,128)(2,1)S(1)} %get-tuple-element.4.blocks_ref, f32[8,8,128]{2,1,0:T(8,128)S(1)} %get-tuple-element.5.spectra_ref), custom_call_target="tpu_custom_call" | custom-call | tf_op jit(solution)/shard_map/normal_maps/pallas_call | solution.py:396

commit v5 on v4

--- a/solution.py
+++ b/solution.py
@@ -18,7 +18,6 @@
 CAP = 4
 ORDERS = 32
 DEG = 96
-PACK = 112
 ROWS = 32
 COLS = 1536
 GROUP = 8
@@ -28,7 +27,7 @@
     orders_ref, legendre_ref, beam_ref, visibility_ref,
     held, spectra,
     orders, legendre, beam, visibility, products, harmonic, outgoing, arrived,
-    crossed, lined,
+    crossed, lined, series, leaving, partials,
     legendre_sem, beam_sem, small_sem, a_send, a_recv, k_send, k_recv, l_send, l_recv, p_send, p_recv,
     x_send, x_recv, c_send, c_recv, s_send, s_recv,
 ):
@@ -40,6 +39,16 @@
     left = ((x + NX - 1) % NX) * 2 + core
     across = ((x + 2) % NX) * 2 + core
     sibling = x * 2 + (1 - core)
+
+    barrier = pltpu.get_barrier_semaphore()
+    for dz in (2, 1, 3, 0):
+        for dy in (2, 1, 3, 0):
+            if dz or dy:
+                peer = ((z + dz) % NZ) * NY + (y + dy) % NY
+                pl.semaphore_signal(barrier, inc=1, device_id={"bl": bl, "ma": peer}, device_id_type=MESH)
+    for d in range(1, 2 * NX):
+        peer = (bl + d) % (2 * NX)
+        pl.semaphore_signal(barrier, inc=1, device_id={"bl": peer, "ma": ma}, device_id_type=MESH)
 
     visibility_load = pltpu.make_async_copy(visibility_ref, visibility, small_sem.at[0])
     visibility_load.start()
@@ -55,14 +64,6 @@
         loads.append(pair)
     orders_load = pltpu.make_async_copy(orders_ref, orders, small_sem.at[1])
     orders_load.start()
-
-    barrier = pltpu.get_barrier_semaphore()
-    for d in range(1, NZ * NY):
-        peer = ((z + d // NY) % NZ) * NY + (y + d) % NY
-        pl.semaphore_signal(barrier, inc=1, device_id={"bl": bl, "ma": peer}, device_id_type=MESH)
-    for d in range(1, 2 * NX):
-        peer = (bl + d) % (2 * NX)
-        pl.semaphore_signal(barrier, inc=1, device_id={"bl": peer, "ma": ma}, device_id_type=MESH)
 
     times = visibility_ref.shape[2]
     total_time = times * NZ * NY
@@ -80,14 +81,10 @@
         lax.dot_general(cosine, direct, contract, precision=lax.Precision.HIGHEST, preferred_element_type=F32)
         + lax.dot_general(sine, turned, contract, precision=lax.Precision.HIGHEST, preferred_element_type=F32)
     ) * (1.0 / math.sqrt(total_time))
-    high = partial.astype(BF16).astype(F32)
-    low = partial - high
-    row = lax.broadcasted_iota(jnp.int32, (PACK - DEG, 128), 0)
     for m in range(ORDERS):
-        harmonic[m, DEG:PACK, :] = jnp.where(
-            row == 0, high[m : m + 1], jnp.where(row == 1, low[m : m + 1], 0.0)
-        ).astype(BF16)
-    harmonic[ORDERS] = jnp.zeros((PACK, 128), BF16)
+        series[m] = jnp.broadcast_to(partial[m : m + 1], (8, 128))
+    series[ORDERS] = jnp.zeros((8, 128), F32)
+    harmonic[ORDERS] = jnp.zeros((DEG, 128), BF16)
 
     part = GROUP // 2
     for g in range(ORDERS // GROUP):
@@ -109,29 +106,27 @@
         pick = (source == wanted + 2 * i).astype(F32).astype(BF16)
         picked = jnp.dot(products[i], pick, preferred_element_type=F32).astype(BF16)
         for g in range(ORDERS // GROUP):
-            harmonic[g * GROUP + i, 0:DEG, :] = picked[g * DEG : (g + 1) * DEG]
+            harmonic[g * GROUP + i] = picked[g * DEG : (g + 1) * DEG]
     orders_load.wait()
 
     pl.semaphore_wait(barrier, NZ * NY - 1 + 2 * NX - 1)
 
-    def row(t, at_y):
-        sign = 1 - 2 * (at_y % 2)
-        return (0, sign, -sign, 2)[t]
+    row = (0, 1, 2, NZ - 1)
 
     def owner_at(t, dy):
-        at_y = (y + dy) % NY
-        return (z + NZ - row(t, at_y)) % NZ, at_y
-
-    slot_lane = lax.broadcasted_iota(jnp.int32, (PACK, 128), 1) // ROWS
+        return (z + NZ - row[t]) % NZ, (y + dy) % NY
+
+    def for_owner(parts):
+        slot = lax.broadcasted_iota(jnp.int32, parts[0].shape, 1) // ROWS
+        return jnp.where(
+            slot < 2,
+            jnp.where(slot == 0, parts[0], parts[1]),
+            jnp.where(slot == 2, parts[2], parts[3]),
+        )
 
     def block_for(at_z, at_y):
         owner = at_z * NY + at_y
-        parts = [harmonic[orders[s, owner]] for s in range(CAP)]
-        return jnp.where(
-            slot_lane < 2,
-            jnp.where(slot_lane == 0, parts[0], parts[1]),
-            jnp.where(slot_lane == 2, parts[2], parts[3]),
-        )
+        return for_owner([harmonic[orders[s, owner]] for s in range(CAP)])
 
     def send(source, target, send_sem, recv_sem, to_bl, to_ma):
         pltpu.make_async_remote_copy(
@@ -145,12 +140,7 @@
     for t in (1, 0):
         for dy in range(NY):
             at_z, at_y = owner_at(t, dy)
-            block = block_for(at_z, at_y)
-            crossed[x, t, at_y] = block[0:DEG]
-            if t or dy:
-                outgoing[t * NY + dy, DEG:PACK] = block[DEG:PACK]
-            else:
-                arrived[ma, DEG:PACK] = block[DEG:PACK]
+            crossed[x, t, at_y] = block_for(at_z, at_y)
         lower, upper = (crossed.at[x, t, pl.ds(h * (NY // 2), NY // 2)] for h in range(2))
         send(lower, lower, k_send, k_recv.at[t, 0], right, ma)
         send(upper, upper, k_send, k_recv.at[t, 1], left, ma)
@@ -158,14 +148,14 @@
         send(lower, lower, k_send, k_recv.at[t, 4], left, ma)
 
     for t in (2, 3):
-        for dy in range(NY):
+        for dy in (2, 1, 3, 0):
             at_z, at_y = owner_at(t, dy)
-            n = t * NY + dy
+            n = (t - 2) * NY + dy
             outgoing[n] = block_for(at_z, at_y)
             send(outgoing.at[n], arrived.at[ma], a_send, a_recv.at[t - 2], bl, at_z * NY + at_y)
 
     def pass_on(t, n, who):
-        for dy in range(NY):
+        for dy in (2, 1, 3, 0):
             if t or dy:
                 at_z, at_y = owner_at(t, dy)
                 send(crossed.at[who // 2, t, at_y], lined.at[t, who // 2, y],
@@ -173,12 +163,14 @@
 
     pass_on(1, 0, bl)
     pass_on(0, 0, bl)
-    for t in (1, 0):
-        for dy in range(NY):
-            if t or dy:
-                at_z, at_y = owner_at(t, dy)
-                send(outgoing.at[t * NY + dy, pl.ds(DEG, PACK - DEG)], arrived.at[ma, pl.ds(DEG, PACK - DEG)],
-                     p_send, p_recv, bl, at_z * NY + at_y)
+    for d in range(NZ * NY):
+        peer = ((z + d // NY) % NZ) * NY + (y + d) % NY
+        line = for_owner([series[orders[s, peer]] for s in range(CAP)])
+        if d == 0:
+            partials[ma] = line
+        else:
+            leaving[d - 1] = line
+            send(leaving.at[d - 1], partials.at[ma], p_send, p_recv, bl, peer)
 
     def cross_near(t):
         half = crossed.at[left // 2, t, pl.ds(0, NY // 2)]
@@ -197,7 +189,7 @@
         pass_on(t, 3, across)
 
     def view(t, who, first=0, count=CAP):
-        return held.at[(z + NZ + row(t, y)) % NZ, who, pl.ds(first, count)]
+        return held.at[(z + row[t]) % NZ, who, pl.ds(first, count)]
 
     def to_sibling(t, who):
         ref = view(t, who)
@@ -205,7 +197,7 @@
 
     def keep(t, who, blocks):
         stacked = jnp.concatenate(blocks, axis=0)
-        held[(z + NZ + row(t, y)) % NZ, who] = stacked.T.reshape(CAP, ROWS, NY * DEG)
+        held[(z + row[t]) % NZ, who] = stacked.T.reshape(CAP, ROWS, NY * DEG)
 
     def collect(t, n, who):
         await_bytes(lined.at[t, 0, pl.ds(0, NY if t else NY - 1)], l_recv.at[t, n])
@@ -216,8 +208,8 @@
 
     def own_part(t):
         await_bytes(arrived.at[pl.ds(0, NY)], a_recv.at[t - 2])
-        at_z = (z + NZ + row(t, y)) % NZ
-        keep(t, bl, [arrived[at_z * NY + j, 0:DEG, :] for j in range(NY)])
+        at_z = (z + row[t]) % NZ
+        keep(t, bl, [arrived[at_z * NY + j] for j in range(NY)])
         lower, upper = (view(t, bl, h * (CAP // 2), CAP // 2) for h in range(2))
         send(lower, lower, x_send, x_recv.at[t - 2, 0], right, ma)
         send(upper, upper, x_send, x_recv.at[t - 2, 1], left, ma)
@@ -249,32 +241,28 @@
     cross_far(0)
     collect(1, 0, bl)
     collect(0, 0, bl)
-
-    await_bytes(arrived.at[pl.ds(0, 2 * NY - 1), pl.ds(DEG, PACK - DEG)], p_recv)
-    total = jnp.zeros((PACK - DEG, 128), F32)
-    for k in range(NZ * NY):
-        total = total + arrived[k, DEG:PACK, :].astype(F32)
-    line = jnp.sum(total, axis=0, keepdims=True).astype(BF16).astype(F32)
+    near_part(2)
+    collect(1, 1, left)
+    collect(1, 2, right)
+    near_part(3)
+    collect(0, 1, left)
+    collect(0, 2, right)
+    await_bytes(leaving, p_recv)
+    line = jnp.sum(partials[...], axis=0)[0:1].astype(BF16).astype(F32)
     spectra[bl] = jnp.broadcast_to(line, (8, 128))
     for d in range(1, 2 * NX):
         send(spectra.at[bl], spectra.at[bl], s_send, s_recv, (bl + d) % (2 * NX), ma)
 
-    collect(1, 1, left)
-    collect(1, 2, right)
-    collect(0, 1, left)
-    collect(0, 2, right)
-    near_part(2)
-    near_part(3)
     collect(1, 3, across)
+    far_part(2)
     collect(0, 3, across)
-    far_part(2)
     far_part(3)
 
     await_bytes(held.at[pl.ds(0, NZ // 2)], c_recv)
     await_bytes(spectra.at[pl.ds(0, 2 * NX - 1)], s_recv)
     await_bytes(crossed.at[pl.ds(0, NX - 1)], k_send)
-    await_bytes(outgoing.at[pl.ds(0, 2 * NY)], a_send)
-    await_bytes(outgoing.at[pl.ds(0, 2 * NY - 1), pl.ds(DEG, PACK - DEG)], p_send)
+    await_bytes(outgoing, a_send)
+    await_bytes(leaving, p_send)
     await_bytes(crossed.at[pl.ds(0, NX - 1), 0], l_send.at[0])
     await_bytes(crossed.at[:, 1], l_send.at[1])
     await_bytes(held.at[0, pl.ds(0, NX + 2)], x_send)
@@ -305,11 +293,14 @@
             pltpu.VMEM(beam.shape, BF16),
             pltpu.VMEM(visibility.shape, F32),
             pltpu.VMEM((GROUP, ORDERS // GROUP * DEG, GROUP * ROWS), BF16),
-            pltpu.VMEM((ORDERS + 1, PACK, 128), BF16),
-            pltpu.VMEM((NZ * NY, PACK, 128), BF16),
-            pltpu.VMEM((NZ * NY, PACK, 128), BF16),
+            pltpu.VMEM((ORDERS + 1, DEG, 128), BF16),
+            pltpu.VMEM((2 * NY, DEG, 128), BF16),
+            pltpu.VMEM((NZ * NY, DEG, 128), BF16),
             pltpu.VMEM((NX, 2, NY, DEG, 128), BF16),
             pltpu.VMEM((2, NX, NY, DEG, 128), BF16),
+            pltpu.VMEM((ORDERS + 1, 8, 128), F32),
+            pltpu.VMEM((NZ * NY - 1, 8, 128), F32),
+            pltpu.VMEM((NZ * NY, 8, 128), F32),
             dma((ORDERS // GROUP,)),
             dma((ORDERS // GROUP,)),
             dma((2,)),

time: 32.1 us -> 31.4 us (0.978)
  the two profiles are of different devices: /device:TPU:25 before, /device:TPU:1 now
where the time goes in v5:
time: 31.4 us; the launch traced here: 31.3 us
  Pallas kernels  30.7 us (98%)
  between operations  0.64 us (2%)
    pallas_call x1, Pallas kernels, gather(): pl.pallas_call(gather_kernel, out_shape=(jax.ShapeDtypeStruct((NZ, 2 * NX...  28 us
    pallas_call x1, Pallas kernels, normal_maps(): pl.pallas_call(normal_kernel, out_shape=(jax.ShapeDtypeStruct((CAP, 2, 19...  2.71 us

profile of v5, /device:TPU:1, one launch (start us, length us, event | category | flops | bytes accessed | tf_op | source)
XLA Modules:
  0.0 31.3 jit_solution(8562960170113901828)
XLA Ops:
  0.6 28.0 %gather_blocks.1 = (bf16[4,8,4,32,384]{4,3,2,1,0:T(8,128)(2,1)S(1)}, f32[8,8,128]{2,1,0:T(8,128)S(1)}) custom-call(s32[4,16]{1,0:T(4,128)} %bitcast.1, bf16[32,96,1024]{2,1,0:T(8,128)(2,1)} %legendre_ref.1, bf16[16,32,2,1024]{3,2,1,0:T(2,128)(2,1)} %beam_ref.1, f32[16,2,256]{2,1,0:T(2,128)} %visibility_ref.1), custom_call_target="tpu_custom_call" | custom-call | tf_op jit(solution)/shard_map/gather_blocks/pallas_call | solution.py:277
  28.6 2.7 %normal_maps.1 = (bf16[4,2,192,1536]{3,2,1,0:T(8,128)(2,1)}, f32[4,2,192]{2,1,0:T(2,128)}) custom-call(bf16[4,8,4,32,384]{4,3,2,1,0:T(8,128)(2,1)S(1)} %get-tuple-element.4.blocks_ref, f32[8,8,128]{2,1,0:T(8,128)S(1)} %get-tuple-element.5.spectra_ref), custom_call_target="tpu_custom_call" | custom-call | tf_op jit(solution)/shard_map/normal_maps/pallas_call | solution.py:387

commit v6 on v5

--- a/solution.py
+++ b/solution.py
@@ -211,26 +211,31 @@
         at_z = (z + row[t]) % NZ
         keep(t, bl, [arrived[at_z * NY + j] for j in range(NY)])
         lower, upper = (view(t, bl, h * (CAP // 2), CAP // 2) for h in range(2))
-        send(lower, lower, x_send, x_recv.at[t - 2, 0], right, ma)
-        send(upper, upper, x_send, x_recv.at[t - 2, 1], left, ma)
-        send(upper, upper, x_send, x_recv.at[t - 2, 3], right, ma)
-        send(lower, lower, x_send, x_recv.at[t - 2, 4], left, ma)
+        for step in range(CAP // 2):
+            ref = view(t, bl, step, 1)
+            send(ref, ref, x_send, x_recv.at[t - 2, 2 * step], right, ma)
+            ref = view(t, bl, CAP - 1 - step, 1)
+            send(ref, ref, x_send, x_recv.at[t - 2, 2 * step + 1], left, ma)
+        send(upper, upper, x_send, x_recv.at[t - 2, 5], right, ma)
+        send(lower, lower, x_send, x_recv.at[t - 2, 6], left, ma)
         to_sibling(t, bl)
 
     def near_part(t):
+        for step in range(CAP // 2):
+            ref = view(t, left, step, 1)
+            await_bytes(ref, x_recv.at[t - 2, 2 * step])
+            send(ref, ref, x_send, x_recv.at[t - 2, 4], right, ma)
+            ref = view(t, right, CAP - 1 - step, 1)
+            await_bytes(ref, x_recv.at[t - 2, 2 * step + 1])
+            send(ref, ref, x_send, x_recv.at[t - 2, 4], left, ma)
         half = view(t, left, 0, CAP // 2)
-        await_bytes(half, x_recv.at[t - 2, 0])
-        send(half, half, x_send, x_recv.at[t - 2, 2], right, ma)
-        half = view(t, right, CAP // 2, CAP // 2)
-        await_bytes(half, x_recv.at[t - 2, 1])
-        send(half, half, x_send, x_recv.at[t - 2, 2], left, ma)
-        await_bytes(half, x_recv.at[t - 2, 3])
+        await_bytes(half, x_recv.at[t - 2, 5])
         to_sibling(t, left)
-        await_bytes(half, x_recv.at[t - 2, 4])
+        await_bytes(half, x_recv.at[t - 2, 6])
         to_sibling(t, right)
 
     def far_part(t):
-        await_bytes(view(t, across), x_recv.at[t - 2, 2])
+        await_bytes(view(t, across), x_recv.at[t - 2, 4])
         to_sibling(t, across)
 
     cross_near(1)
@@ -313,7 +318,7 @@
             dma,
             dma,
             dma,
-            dma((2, 5)),
+            dma((2, 7)),
             dma,
             dma,
             dma,

time: 31.4 us -> 31.5 us (level)
  no operation moved by 1% of the time
where the time goes in v6:
time: 31.5 us; the launch traced here: 31.4 us
  Pallas kernels  30.7 us (97%)
  between operations  0.64 us (2%)
    pallas_call x1, Pallas kernels, gather(): pl.pallas_call(gather_kernel, out_shape=(jax.ShapeDtypeStruct((NZ, 2 * NX...  28 us
    pallas_call x1, Pallas kernels, normal_maps(): pl.pallas_call(normal_kernel, out_shape=(jax.ShapeDtypeStruct((CAP, 2, 19...  2.71 us

profile of v6, /device:TPU:1, one launch (start us, length us, event | category | flops | bytes accessed | tf_op | source)
XLA Modules:
  0.0 31.4 jit_solution(12418471566063338587)
XLA Ops:
  0.6 28.0 %gather_blocks.1 = (bf16[4,8,4,32,384]{4,3,2,1,0:T(8,128)(2,1)S(1)}, f32[8,8,128]{2,1,0:T(8,128)S(1)}) custom-call(s32[4,16]{1,0:T(4,128)} %bitcast.1, bf16[32,96,1024]{2,1,0:T(8,128)(2,1)} %legendre_ref.1, bf16[16,32,2,1024]{3,2,1,0:T(2,128)(2,1)} %beam_ref.1, f32[16,2,256]{2,1,0:T(2,128)} %visibility_ref.1), custom_call_target="tpu_custom_call" | custom-call | tf_op jit(solution)/shard_map/gather_blocks/pallas_call | solution.py:282
  28.7 2.7 %normal_maps.1 = (bf16[4,2,192,1536]{3,2,1,0:T(8,128)(2,1)}, f32[4,2,192]{2,1,0:T(2,128)}) custom-call(bf16[4,8,4,32,384]{4,3,2,1,0:T(8,128)(2,1)S(1)} %get-tuple-element.4.blocks_ref, f32[8,8,128]{2,1,0:T(8,128)S(1)} %get-tuple-element.5.spectra_ref), custom_call_target="tpu_custom_call" | custom-call | tf_op jit(solution)/shard_map/normal_maps/pallas_call | solution.py:392

commit v7 on v5

--- a/solution.py
+++ b/solution.py
@@ -155,7 +155,7 @@
             send(outgoing.at[n], arrived.at[ma], a_send, a_recv.at[t - 2], bl, at_z * NY + at_y)
 
     def pass_on(t, n, who):
-        for dy in (2, 1, 3, 0):
+        for dy in (0, 1, 2, 3):
             if t or dy:
                 at_z, at_y = owner_at(t, dy)
                 send(crossed.at[who // 2, t, at_y], lined.at[t, who // 2, y],

time: 31.4 us -> 31.4 us (level)
  no operation moved by 1% of the time
where the time goes in v7:
time: 31.4 us; the launch traced here: 31.3 us
  Pallas kernels  30.7 us (98%)
  between operations  0.64 us (2%)
    pallas_call x1, Pallas kernels, gather(): pl.pallas_call(gather_kernel, out_shape=(jax.ShapeDtypeStruct((NZ, 2 * NX...  28 us
    pallas_call x1, Pallas kernels, normal_maps(): pl.pallas_call(normal_kernel, out_shape=(jax.ShapeDtypeStruct((CAP, 2, 19...  2.71 us

profile of v7, /device:TPU:1, one launch (start us, length us, event | category | flops | bytes accessed | tf_op | source)
XLA Modules:
  0.0 31.3 jit_solution(14550003044847461531)
XLA Ops:
  0.6 28.0 %gather_blocks.1 = (bf16[4,8,4,32,384]{4,3,2,1,0:T(8,128)(2,1)S(1)}, f32[8,8,128]{2,1,0:T(8,128)S(1)}) custom-call(s32[4,16]{1,0:T(4,128)} %bitcast.1, bf16[32,96,1024]{2,1,0:T(8,128)(2,1)} %legendre_ref.1, bf16[16,32,2,1024]{3,2,1,0:T(2,128)(2,1)} %beam_ref.1, f32[16,2,256]{2,1,0:T(2,128)} %visibility_ref.1), custom_call_target="tpu_custom_call" | custom-call | tf_op jit(solution)/shard_map/gather_blocks/pallas_call | solution.py:277
  28.6 2.7 %normal_maps.1 = (bf16[4,2,192,1536]{3,2,1,0:T(8,128)(2,1)}, f32[4,2,192]{2,1,0:T(2,128)}) custom-call(bf16[4,8,4,32,384]{4,3,2,1,0:T(8,128)(2,1)S(1)} %get-tuple-element.4.blocks_ref, f32[8,8,128]{2,1,0:T(8,128)S(1)} %get-tuple-element.5.spectra_ref), custom_call_target="tpu_custom_call" | custom-call | tf_op jit(solution)/shard_map/normal_maps/pallas_call | solution.py:387
